TPU v7x, 256 devices: a whole 4x4x8 slice. The times are simulated.
256 devices in a mesh: dp: 64 (over z, y, core), mp: 4 (over x).
Axes of the slice: x: 4, y: 4, z: 8, core: 2. Of those that a mesh axis runs over, the one named last changes fastest.
Arguments:
- queries: bfloat16 [8192, 64, 576], P('dp', 'mp'), may hold values from -17 to 17
- latents: bfloat16 [8192, 576], P('dp'), may hold values from -6 to 6
- doc_ids: int32 [8192], replicated, may hold values from 0 to 127, never falling along the last dimension, each value on 1 to 128 neighbouring positions
- hidden_rows: bfloat16 [8192, 5120], P('dp', 'mp'), may hold values from -6 to 6
- expert_ids: int32 [8192, 6], P('dp'), may hold values from 0 to 31, all different within a row; in each aligned block of 128 rows (0 to 127, 128 to 255, ...) at most 30 rows name the same one
- gate_scores: float32 [8192, 6], P('dp'), may hold values from 0.05 to 0.6
- gate_weight: bfloat16 [64, 2560, 1536], P('dp', None, 'mp'), may hold values from -0.078125 to 0.078125
- up_weight: bfloat16 [64, 2560, 1536], P('dp', None, 'mp'), may hold values from -0.078125 to 0.078125
- down_weight: bfloat16 [64, 1536, 2560], P('dp', 'mp'), may hold values from -0.15625 to 0.15625
Outputs:
- attn_out: bfloat16 [8192, 64, 512], P('dp', 'mp')
- moe_out: bfloat16 [8192, 5120], P('dp', 'mp')
Inputs may be any that keep to these rules, and one draw needn't show every extreme that they name: `doc_ids`: document numbers never fall along the tokens; every document has 1 to 128 tokens. `expert_ids`: each token names 6 different experts; no expert is named by more than 30 tokens of one aligned block of 128 tokens.
All inputs are finite; a program needn't handle non-finite values.
Results may differ from a plain program's by a relative error of at most 0.015.
Values may be sent and summed in bfloat16 or wider, within the bound.
A program may use at most 128 MiB of HBM per device.

v0:
```python
import math

import jax
import jax.numpy as jnp
from jax import lax
from jax.sharding import PartitionSpec as P

TOP = 6
LAT = 512


score_scale = 1.0 / math.sqrt(192.0)
neg_large = -1e30


def from_partner(shard, axis, stride):
    return lax.ppermute(shard, axis, [(i, i ^ 1 << stride) for i in range(lax.axis_size(axis))])


def passed_along(shard, axis, by):
    length = lax.axis_size(axis)
    pairs = [(i, i + by) for i in range(length) if 0 <= i + by < length]
    return lax.ppermute(shard, axis, pairs)


def softmax_rows(scores, allowed):
    masked = jnp.where(allowed, scores, neg_large)
    row_top = jnp.max(masked, axis=-1, keepdims=True)
    lifted = jnp.where(allowed, jnp.exp(masked - row_top), 0.0)
    return (lifted / jnp.sum(lifted, axis=-1, keepdims=True)).astype(jnp.bfloat16)


def weigh_routes(merged, gate_scores, route_places):
    total = jnp.zeros((route_places.shape[0], merged.shape[1]), jnp.float32)
    for route in range(route_places.shape[1]):
        total = total + gate_scores[:, route : route + 1] * merged[route_places[:, route]].astype(
            jnp.float32
        )
    return total


def shards(
    queries,
    latents,
    doc_ids,
    hidden_rows,
    expert_ids,
    gate_scores,
    gate_weight,
    up_weight,
    down_weight,
):
    tok_rows = latents.shape[0]
    dp_count = lax.axis_size("dp")
    mp_count = lax.axis_size("mp")
    my_index = lax.axis_index("dp")
    other_gate, other_up, other_down = from_partner(
        (gate_weight[0], up_weight[0], down_weight[0]), "dp", 0
    )
    previous = passed_along(latents, "dp", 1)
    keys = jnp.concatenate([previous, latents], 0)
    start = my_index * tok_rows
    padded_ids = jnp.concatenate([jnp.full((tok_rows,), -1, jnp.int32), doc_ids], 0)
    key_ids = lax.dynamic_slice_in_dim(padded_ids, start, 2 * tok_rows, 0)
    query_ids = lax.dynamic_slice_in_dim(doc_ids, start, tok_rows, 0)
    query_pos = jnp.arange(tok_rows, dtype=jnp.int32) + tok_rows
    key_pos = jnp.arange(2 * tok_rows, dtype=jnp.int32)
    allowed = (query_ids[:, None] == key_ids[None, :]) & (key_pos[None, :] <= query_pos[:, None])
    scores = (
        jnp.einsum("thf,uf->thu", queries, keys, preferred_element_type=jnp.float32) * score_scale
    )
    probs = softmax_rows(scores, allowed[:, None, :])
    attn_out = jnp.einsum(
        "thu,uf->thf", probs, keys[:, :LAT], preferred_element_type=jnp.float32
    ).astype(jnp.bfloat16)
    full_rows = lax.all_gather(hidden_rows, "mp", axis=1, tiled=True)
    width = full_rows.shape[1]
    experts = dp_count // 2
    capacity = 2 * ((5 * tok_rows * TOP + 8 * experts - 1) // (8 * experts))
    routes = expert_ids.reshape(-1)
    onehot = (routes[:, None] == jnp.arange(experts, dtype=jnp.int32)[None, :]).astype(jnp.int32)
    earlier = jnp.cumsum(onehot, axis=0) - onehot
    slots = jnp.sum(earlier * onehot, axis=1)
    places = routes * capacity + slots
    owners = jnp.arange(routes.shape[0], dtype=jnp.int32) // TOP
    table = jnp.full((experts * capacity,), -1, jnp.int32).at[places].set(owners)
    safe = jnp.maximum(table, 0)
    outgoing = full_rows[safe].reshape(dp_count, capacity // 2, width)
    is_first = my_index % 2 == 0
    gate_full = jnp.concatenate(
        [
            jnp.where(is_first, gate_weight[0], other_gate),
            jnp.where(is_first, other_gate, gate_weight[0]),
        ],
        0,
    )
    up_full = jnp.concatenate(
        [jnp.where(is_first, up_weight[0], other_up), jnp.where(is_first, other_up, up_weight[0])],
        0,
    )
    hidden_dev = gate_weight.shape[2]
    piece = width // 2 // mp_count
    down_sets = jnp.stack(
        [
            jnp.where(is_first, down_weight[0], other_down),
            jnp.where(is_first, other_down, down_weight[0]),
        ],
        0,
    )
    down_full = (
        down_sets.reshape(2, hidden_dev, mp_count, piece)
        .transpose(1, 2, 0, 3)
        .reshape(hidden_dev, width)
    )
    block = lax.all_to_all(outgoing, "dp", split_axis=0, concat_axis=0, tiled=True)
    sources = block.shape[0]
    items = block.shape[1]
    rows = block.reshape(sources * items, width)
    gate_part = jnp.dot(rows, gate_full, preferred_element_type=jnp.float32)
    up_part = jnp.dot(rows, up_full, preferred_element_type=jnp.float32)
    hidden = (jax.nn.silu(gate_part) * up_part).astype(jnp.bfloat16)
    partial_value = jnp.dot(hidden, down_full, preferred_element_type=jnp.float32).astype(
        jnp.bfloat16
    )
    returned = partial_value.reshape(sources, items, width)
    route_places = places.reshape(tok_rows, TOP)
    back = lax.all_to_all(returned, "dp", split_axis=0, concat_axis=0, tiled=True)
    merged = back.reshape(experts * capacity, width)
    combined = weigh_routes(merged, gate_scores, route_places)
    moe_out = lax.psum_scatter(combined.astype(jnp.bfloat16), "mp", scatter_dimension=1, tiled=True)
    return (attn_out, moe_out)


def solution(mesh):
    placed = (
        P("dp", "mp", None),
        P("dp", None),
        P(),
        P("dp", "mp"),
        P("dp", None),
        P("dp", None),
        P("dp", None, "mp"),
        P("dp", None, "mp"),
        P("dp", "mp", None),
    )
    return jax.shard_map(
        shards,
        mesh=mesh,
        in_specs=placed,
        out_specs=(P("dp", "mp", None), P("dp", "mp")),
        check_vma=False,
    )
```

profile of v0, /device:TPU:16, one launch (start us, length us, event | category | flops | bytes accessed | tf_op | source)
XLA Modules:
  0.0 705.0 jit_solution(15467264177993500263)
XLA Ops:
  7.2 0.7 all-gather.2.cloned.1.call-update
  7.9 0.8 copy.25
  8.7 0.1 eq.54
  8.8 0.1 eq.50
  9.0 1.7 reduce-window.6
  10.7 0.3 slice_reduce_fusion
  11.0 0.1 fusion.24
  11.2 0.1 reduce_sum.25
  11.3 0.1 mul.107
  11.5 3.4 scatter_custom_fusion
  14.9 25.2 %all-gather.2.cloned.1.call-done = bf16[128,5120]{1,0:T(8,128)(2,1)} async-done(((bf16[128,1280]{1,0:T(8,128)(2,1)}), bf16[128,5120]{1,0:T(8,128)(2,1)}) %all-gather.2.cloned.1.call-update) | async-done | bytes 1310736 | tf_op jit(solution)/shard_map/all_gather | solution.py:76
  40.1 19.8 %gather_fusion = bf16[960,5120]{1,0:T(8,128)(2,1)} fusion(bf16[128,5120]{1,0:T(8,128)(2,1)} %all-gather.2.cloned.1.call-done, s32[1024]{0:T(1024)S(1)} %pad_clamp_fusion.6), kind=kCustom, calls=%fused_computation | custom fusion | bytes 19664640 | tf_op jit(solution)/shard_map/gather | solution.py:88
  59.9 11.0 %reshape.120 = bf16[64,15,5120]{2,1,0:T(8,128)(2,1)} reshape(bf16[960,5120]{1,0:T(8,128)(2,1)} %gather_fusion) | data formatting | bytes 19660800 | tf_op jit(solution)/shard_map/reshape | solution.py:88
  70.9 10.7 %all-to-all-start = ((bf16[64,15,5120]{2,1,0:T(8,128)(2,1)}), bf16[64,15,5120]{2,1,0:T(8,128)(2,1)}, u32[]{:S(2)}, u32[]{:S(2)}) async-start(bf16[64,15,5120]{2,1,0:T(8,128)(2,1)} %reshape.120), calls=%async_computation | async-start | bytes 20971520 | tf_op jit(solution)/shard_map/all_to_all | solution.py:115
  81.6 0.2 collective-permute-start.3
  81.9 0.4 collective-permute-start.1
  82.2 0.7 collective-permute-start.2
  82.9 3.2 collective-permute-done.3
  86.0 4.3 broadcast_select_fusion.1
  90.3 4.0 copy.29
  94.3 3.9 copy.30
  98.3 4.6 pad_maximum_fusion
  102.9 4.0 broadcast_select_fusion.5
  106.8 3.9 broadcast_select_fusion.3
  110.8 198.8 %all-to-all-done = bf16[64,15,5120]{2,1,0:T(8,128)(2,1)} async-done(((bf16[64,15,5120]{2,1,0:T(8,128)(2,1)}), bf16[64,15,5120]{2,1,0:T(8,128)(2,1)}, u32[]{:S(2)}, u32[]{:S(2)}) %all-to-all-start) | async-done | bytes 9830432 | tf_op jit(solution)/shard_map/all_to_all | solution.py:115
  309.5 11.1 %reshape.121 = bf16[960,5120]{1,0:T(8,128)(2,1)} reshape(bf16[64,15,5120]{2,1,0:T(8,128)(2,1)} %all-to-all-done) | data formatting | bytes 19660800 | tf_op jit(solution)/shard_map/reshape | solution.py:118
  320.6 10.0 %fusion.1 = f32[960,384]{1,0:T(8,128)} fusion(bf16[960,5120]{1,0:T(8,128)(2,1)} %reshape.121, bf16[2560,384]{1,0:T(8,128)(2,1)} %get-tuple-element.17, bf16[2560,384]{1,0:T(8,128)(2,1)} %get-tuple-element.16), kind=kOutput, calls=%fused_computation.10 | convolution fusion | flops 3782737920 | bytes 15237120 | tf_op jit(solution)/shard_map/dot_general | solution.py:119
  330.6 17.7 %convolution_convert_fusion = bf16[960,5120]{1,0:T(8,128)(2,1)} fusion(bf16[384,5120]{0,1:T(8,128)(2,1)} %bitcast.69, f32[960,384]{1,0:T(8,128)} %fusion.1, bf16[960,5120]{1,0:T(8,128)(2,1)} %reshape.121, bf16[2560,384]{1,0:T(8,128)(2,1)} %get-tuple-element.15, bf16[2560,384]{1,0:T(8,128)(2,1)} %get-tuple-element.14), kind=kOutput, calls=%fused_computation.9 | convolution fusion | flops 7564738560 | bytes 28999680 | tf_op jit(solution)/shard_map/dot_general | solution.py:122
  348.3 11.0 %reshape.123 = bf16[64,15,5120]{2,1,0:T(8,128)(2,1)} reshape(bf16[960,5120]{1,0:T(8,128)(2,1)} %convolution_convert_fusion) | data formatting | bytes 19660800 | tf_op jit(solution)/shard_map/reshape | solution.py:125
  359.3 11.7 %all-to-all-start.1 = ((bf16[64,15,5120]{2,1,0:T(8,128)(2,1)}), bf16[64,15,5120]{2,1,0:T(8,128)(2,1)}, u32[]{:S(2)}, u32[]{:S(2)}) async-start(bf16[64,15,5120]{2,1,0:T(8,128)(2,1)} %reshape.123), calls=%async_computation.1 | async-start | bytes 20971520 | tf_op jit(solution)/shard_map/all_to_all | solution.py:127
  371.0 0.3 fusion.26
  371.4 227.5 %all-to-all-done.1 = bf16[64,15,5120]{2,1,0:T(8,128)(2,1)} async-done(((bf16[64,15,5120]{2,1,0:T(8,128)(2,1)}), bf16[64,15,5120]{2,1,0:T(8,128)(2,1)}, u32[]{:S(2)}, u32[]{:S(2)}) %all-to-all-start.1) | async-done | bytes 9830432 | tf_op jit(solution)/shard_map/all_to_all | solution.py:127
  598.9 11.2 %reshape.124 = bf16[960,5120]{1,0:T(8,128)(2,1)} reshape(bf16[64,15,5120]{2,1,0:T(8,128)(2,1)} %all-to-all-done.1) | data formatting | bytes 19660800 | tf_op jit(solution)/shard_map/reshape | solution.py:128
  610.1 8.8 %gather_fusion.1 = bf16[128,5120]{1,0:T(8,128)(2,1)} fusion(bf16[960,5120]{1,0:T(8,128)(2,1)} %reshape.124, s32[1024]{0:T(1024)S(1)} %get-tuple-element.35), kind=kCustom, calls=%fused_computation.1 | custom fusion | bytes 2621952 | tf_op jit(solution)/shard_map/gather | solution.py:36
  618.9 8.7 %gather_fusion.2 = bf16[128,5120]{1,0:T(8,128)(2,1)} fusion(bf16[960,5120]{1,0:T(8,128)(2,1)} %reshape.124, s32[1024]{0:T(1024)S(1)} %get-tuple-element.34), kind=kCustom, calls=%fused_computation.2 | custom fusion | bytes 2621952 | tf_op jit(solution)/shard_map/gather | solution.py:36
  627.6 8.7 %gather_fusion.3 = bf16[128,5120]{1,0:T(8,128)(2,1)} fusion(bf16[960,5120]{1,0:T(8,128)(2,1)} %reshape.124, s32[1024]{0:T(1024)S(1)} %get-tuple-element.33), kind=kCustom, calls=%fused_computation.3 | custom fusion | bytes 2621952 | tf_op jit(solution)/shard_map/gather | solution.py:36
  636.4 8.9 %gather_fusion.4 = bf16[128,5120]{1,0:T(8,128)(2,1)} fusion(bf16[960,5120]{1,0:T(8,128)(2,1)} %reshape.124, s32[1024]{0:T(1024)S(1)} %get-tuple-element.32), kind=kCustom, calls=%fused_computation.4 | custom fusion | bytes 2621952 | tf_op jit(solution)/shard_map/gather | solution.py:36
  645.3 8.8 %gather_fusion.5 = bf16[128,5120]{1,0:T(8,128)(2,1)} fusion(bf16[960,5120]{1,0:T(8,128)(2,1)} %reshape.124, s32[1024]{0:T(1024)S(1)} %get-tuple-element.31), kind=kCustom, calls=%fused_computation.5 | custom fusion | bytes 2621952 | tf_op jit(solution)/shard_map/gather | solution.py:36
  654.1 8.7 %gather_fusion.6 = bf16[128,5120]{1,0:T(8,128)(2,1)} fusion(bf16[960,5120]{1,0:T(8,128)(2,1)} %reshape.124, s32[1024]{0:T(1024)S(1)} %get-tuple-element.30), kind=kCustom, calls=%fused_computation.6 | custom fusion | bytes 2621952 | tf_op jit(solution)/shard_map/gather | solution.py:36
  662.8 6.4 add_convert_fusion
  669.2 2.2 collective-permute-start
  671.4 0.1 dynamic_slice.6
  671.6 0.1 fusion.21
  671.7 5.8 collective-permute-done
  677.6 2.8 fusion.45
  680.3 2.4 convolution_convert_fusion.1
  682.7 2.5 copy.31
  685.2 12.7 %reduce-scatter.2.cloned.1.call-done = bf16[128,1280]{1,0:T(8,128)(2,1)} async-done(((bf16[128,5120]{1,0:T(8,128)(2,1)}), bf16[128,1280]{1,0:T(8,128)(2,1)}) %reduce-scatter.2.cloned.1.call-update) | async-done | bytes 327696 | tf_op jit(solution)/shard_map/reduce_scatter | solution.py:130
  (32 shorter events, 0.4 us)
Async XLA Ops:
  7.2 670.4 %copy-start = (bf16[128,16,576]{0,2,1:T(8,128)(2,1)S(1)}, bf16[128,16,576]{0,2,1:T(8,128)(2,1)}, u32[]{:S(2)}) copy-start(bf16[128,16,576]{0,2,1:T(8,128)(2,1)} %param.9) | copy-start | bytes 7077892
  7.2 32.9 %all-gather.2.cloned.1.call-start = ((), (), s32[]{:S(2)}) async-start(), calls=%async_computation.3 | async-start | bytes 1638400 | tf_op jit(solution)/shard_map/all_gather | solution.py:76
  70.9 238.6 %all-to-all-start = ((bf16[64,15,5120]{2,1,0:T(8,128)(2,1)}), bf16[64,15,5120]{2,1,0:T(8,128)(2,1)}, u32[]{:S(2)}, u32[]{:S(2)}) async-start(bf16[64,15,5120]{2,1,0:T(8,128)(2,1)} %reshape.120), calls=%async_computation | async-start | bytes 20971520 | tf_op jit(solution)/shard_map/all_to_all | solution.py:115
  81.6 4.4 collective-permute-start.3
  81.9 21.0 %collective-permute-start.1 = (bf16[2560,384]{1,0:T(8,128)(2,1)}, bf16[2560,384]{1,0:T(8,128)(2,1)}, u32[]{:S(2)}, u32[]{:S(2)}) collective-permute-start(bf16[2560,384]{1,0:T(8,128)(2,1)} %bitcast.71), channel_id=1, source_target_pairs={{0,4},{4,0},{8,12},{12,8},{16,20},{20,16},{24,28},{28,24},{32,36},... | collective-permute-start | bytes 5898248 | tf_op jit(solution)/shard_map/ppermute | solution.py:17
  82.2 24.6 %collective-permute-start.2 = (bf16[2560,384]{1,0:T(8,128)(2,1)}, bf16[2560,384]{1,0:T(8,128)(2,1)}, u32[]{:S(2)}, u32[]{:S(2)}) collective-permute-start(bf16[2560,384]{1,0:T(8,128)(2,1)} %bitcast.72), channel_id=1, source_target_pairs={{0,4},{4,0},{8,12},{12,8},{16,20},{20,16},{24,28},{28,24},{32,36},... | collective-permute-start | bytes 5898248 | tf_op jit(solution)/shard_map/ppermute | solution.py:17
  98.3 4.6 copy-start.1
  102.9 4.0 copy-start.2
  359.3 12.1 %copy-start.5 = (f32[128,6]{0,1:T(8,128)S(1)}, f32[128,6]{0,1:T(8,128)}, u32[]{:S(2)}) copy-start(f32[128,6]{0,1:T(8,128)} %param.14) | copy-start | bytes 9220
  359.3 239.6 %all-to-all-start.1 = ((bf16[64,15,5120]{2,1,0:T(8,128)(2,1)}), bf16[64,15,5120]{2,1,0:T(8,128)(2,1)}, u32[]{:S(2)}, u32[]{:S(2)}) async-start(bf16[64,15,5120]{2,1,0:T(8,128)(2,1)} %reshape.123), calls=%async_computation.1 | async-start | bytes 20971520 | tf_op jit(solution)/shard_map/all_to_all | solution.py:127
  371.0 326.9 %reduce-scatter.2.cloned.1.call-start = ((), (), s32[]{:S(2)}) async-start(), calls=%async_computation.4 | async-start | bytes 1638400 | tf_op jit(solution)/shard_map/reduce_scatter | solution.py:130
  662.8 6.4 copy-start.3
  662.8 8.6 %copy-start.4 = (s32[8192]{0:T(1024)S(1)}, s32[8192]{0:T(1024)}, u32[]{:S(2)}) copy-start(s32[8192]{0:T(1024)} %param.11) | copy-start | bytes 98308
  669.2 8.3 %collective-permute-start = (bf16[128,576]{0,1:T(8,128)(2,1)S(1)}, bf16[128,576]{0,1:T(8,128)(2,1)S(1)}, u32[]{:S(2)}, u32[]{:S(2)}) collective-permute-start(bf16[128,576]{0,1:T(8,128)(2,1)S(1)} %copy-done.3), channel_id=1, source_target_pairs={{0,4},{4,8},{8,12},{12,16},{16,20},{20,24},{24,28},{28,32},{32,36}... | collective-permute-start | bytes 442376 | tf_op jit(solution)/shard_map/ppermute | solution.py:23
Sparse Core Ops, SparseCore 0:
  9.8 30.2 all-gather.1
  669.3 28.5 reduce-scatter.1
where the time goes:
time: 712 us; the launch traced here: 705 us
  waiting for transfers between devices  474 us (67%)
  local copies, waits for them, and re-layouts  132 us (19%)
  matrix products  32.8 us (5%)
  starting transfers between devices  25.9 us (4%)
  other arithmetic  25.5 us (4%)
  between operations  14.5 us (2%)
    all_to_all x1, waiting for transfers between devices, shards(): lax.all_to_all(returned, 'dp', split_axis=0, concat_axis=0, tiled=True)  227 us
    all_to_all x1, waiting for transfers between devices, shards(): lax.all_to_all(outgoing, 'dp', split_axis=0, concat_axis=0, tiled=True)  199 us
    gather x6, local copies, waits for them, and re-layouts, weigh_routes(): merged[route_places[:, route]].astype(jnp.float32)  52.7 us
    all_gather x1, waiting for transfers between devices, shards(): full_rows = lax.all_gather(hidden_rows, 'mp', axis=1, tiled=True)  25.2 us
    gather x1, local copies, waits for them, and re-layouts, shards(): outgoing = full_rows[safe].reshape(dp_count, capacity // 2, width)  19.8 us
    dot_general x1, matrix products, shards(): jnp.dot(hidden, down_full, preferred_element_type=jnp.float32)  17.7 us
  transfers between devices with their start and end apart: 8, of which 6 were waited for; matrix products, arithmetic and copies ran while one was open for 6% of the time, Pallas kernels for 0%

commit v1 on v0

v1 whole, which is shorter than its diff:
```python
import functools
import math

import jax
import jax.numpy as jnp
from jax import lax
from jax.experimental import pallas as pl
from jax.experimental.pallas import tpu as pltpu
from jax.sharding import PartitionSpec as P

LAT = 512
SLOTS = 32
NX = 4
NY = 4
Z_ORDER = {8: (1, -2, 2, -3, 3, 4, -1, 0), 4: (1, 2, -1, 0), 2: (1, 0)}

score_scale = 1.0 / math.sqrt(192.0)
neg_large = -1e30
MESH = pl.DeviceIdType.MESH


def layer_kernel(
    nz,
    ny,
    ids_ref,
    score_ref,
    tok_ref,
    gate_ref,
    up_ref,
    down_ref,
    query_ref,
    latent_ref,
    doc_ref,
    out_ref,
    attn_ref,
    disp,
    rows,
    gu,
    dn,
    relay_dn,
    hid,
    outb,
    ret,
    acc,
    place_ref,
    ghi_ref,
    glo_ref,
    query,
    attn,
    keys,
    bias,
    local_sem,
    q_sem,
    lat_send,
    lat_recv,
    w_send,
    w_recv,
    disp_send,
    disp_recv,
    x_send,
    x_recv,
    h_send,
    h_recv,
    ret_send,
    ret_recv,
):
    top, tokens = ids_ref.shape
    heads = query_ref.shape[0]
    width = tok_ref.shape[1]
    half_in, units = gate_ref.shape
    piece = down_ref.shape[1] // NX
    experts = nz * ny
    chunk = ny * SLOTS
    half = chunk // 2
    f32, bf16 = jnp.float32, jnp.bfloat16

    d = lax.axis_index("dp")
    x = lax.axis_index("mp")
    s = lax.rem(d, 2)
    p = lax.div(d, 2)
    z = lax.div(p, ny)
    y = lax.rem(p, ny)
    right = lax.rem(x + 1, NX)
    left = lax.rem(x + NX - 1, NX)
    opposite = lax.rem(x + 2, NX)
    mate = d + 1 - 2 * s

    def dev(zz, yy):
        return (zz * ny + yy) * 2 + s

    def offset(c):
        total = 0
        for at, by in enumerate(Z_ORDER[nz]):
            total = total + jnp.where(c == at, by, 0)
        return total

    def remote(src, dst, send, recv, dd, xx):
        return pltpu.make_async_remote_copy(
            src_ref=src, dst_ref=dst, send_sem=send, recv_sem=recv,
            device_id=(dd, xx), device_id_type=MESH,
        )

    def wait_in(ref, sem):
        pltpu.make_async_copy(ref, ref, sem).wait()

    own_in = pl.ds(pl.multiple_of(s * half_in, half_in), half_in)
    mate_in = pl.ds(pl.multiple_of((1 - s) * half_in, half_in), half_in)
    own_out = pl.ds(pl.multiple_of(s * piece, piece), piece)
    mate_out = pl.ds(pl.multiple_of((1 - s) * piece, piece), piece)
    gate_cols, up_cols = pl.ds(0, units), pl.ds(units, units)

    def unit_rows(q, start, count):
        return pl.ds(pl.multiple_of(q * units + start, units // 2), count)

    def unit_cols(q):
        return pl.ds(pl.multiple_of(q * units, units), units)

    def down_cols(q):
        return pl.ds(pl.multiple_of(q * piece, piece), piece)

    local_gate = pltpu.make_async_copy(gate_ref, gu.at[own_in, gate_cols], local_sem.at[0])
    local_up = pltpu.make_async_copy(up_ref, gu.at[own_in, up_cols], local_sem.at[1])
    local_down = pltpu.make_async_copy(
        down_ref.at[:, down_cols(x)], dn.at[unit_rows(x, 0, units), own_out], local_sem.at[2]
    )
    local_gate.start()
    local_up.start()
    local_down.start()
    local_query = pltpu.make_async_copy(query_ref, query, q_sem.at[0])
    local_query.start()

    barrier = pltpu.get_barrier_semaphore()

    def greet(dd, xx):
        pl.semaphore_signal(barrier, inc=1, device_id=(dd, xx), device_id_type=MESH)

    ring = experts * 2
    beside = lax.rem(d + 2 * s - 1 + ring, ring)
    following = lax.rem(d + 1, ring)
    greet(mate, x)
    greet(beside, x)
    greet(d, right)
    greet(d, left)

    def greet_peer(k, carry):
        greet(lax.rem(p + k, experts) * 2 + s, x)
        return carry

    lax.fori_loop(1, experts, greet_peer, 0)

    expert_at = lax.broadcasted_iota(jnp.int32, (experts, tokens), 0)
    named = jnp.zeros((experts, tokens), f32)
    weight = jnp.zeros((experts, tokens), f32)
    for k in range(top):
        hit = ids_ref[k : k + 1, :] == expert_at
        named = named + jnp.where(hit, 1.0, 0.0)
        weight = weight + jnp.where(hit, score_ref[k : k + 1, :], 0.0)
    row_at = lax.broadcasted_iota(jnp.int32, (tokens, tokens), 0)
    col_at = lax.broadcasted_iota(jnp.int32, (tokens, tokens), 1)
    before = jnp.dot(
        named.astype(bf16),
        jnp.where(row_at < col_at, 1.0, 0.0).astype(bf16),
        preferred_element_type=f32,
    )
    place_ref[...] = jnp.where(named > 0.5, before, -1.0).astype(bf16)
    whole = weight.astype(bf16)
    ghi_ref[...] = whole
    glo_ref[...] = (weight - whole.astype(f32)).astype(bf16)

    same = row_at == col_at
    keys[tokens:, :] = lax.dot_general(
        jnp.where(same, 1.0, 0.0).astype(bf16), latent_ref[...], (((1,), (1,)), ((), ())),
        preferred_element_type=f32,
    ).astype(bf16)
    lat_copy = remote(
        keys.at[pl.ds(tokens, tokens)], keys.at[pl.ds(0, tokens)],
        lat_send.at[0], lat_recv.at[0], following, x,
    )
    own_ids = doc_ref[pl.ds(d, 1), :]
    old_ids = doc_ref[pl.ds(lax.rem(d + ring - 1, ring), 1), :]
    own_col = jnp.sum(jnp.where(same, own_ids, 0).astype(f32), axis=1, keepdims=True)
    old_col = jnp.sum(jnp.where(same, old_ids, 0).astype(f32), axis=1, keepdims=True)
    old_col = old_col - jnp.where(d == 0, 1000.0, 0.0)
    ids_row = own_ids.astype(f32)
    bias[:tokens, :] = jnp.where(old_col == ids_row, 0.0, neg_large)
    bias[tokens:, :] = jnp.where((own_col == ids_row) & (row_at <= col_at), 0.0, neg_large)

    pl.semaphore_wait(barrier, experts - 1 + 4)

    to_mate = [
        remote(gate_ref, gu.at[own_in, gate_cols], w_send.at[0], w_recv.at[0], mate, x),
        remote(up_ref, gu.at[own_in, up_cols], w_send.at[1], w_recv.at[1], mate, x),
    ]
    halfu = units // 2
    to_side = [
        remote(
            down_ref.at[:, down_cols(right)], dn.at[unit_rows(x, 0, units), own_out],
            w_send.at[2], w_recv.at[2], d, right,
        ),
        remote(
            down_ref.at[:, down_cols(left)], dn.at[unit_rows(x, 0, units), own_out],
            w_send.at[3], w_recv.at[3], d, left,
        ),
        remote(
            down_ref.at[pl.ds(0, halfu), down_cols(opposite)], relay_dn.at[0],
            w_send.at[4], w_recv.at[4], d, right,
        ),
        remote(
            down_ref.at[pl.ds(halfu, halfu), down_cols(opposite)], relay_dn.at[1],
            w_send.at[5], w_recv.at[5], d, left,
        ),
    ]
    relays = [
        remote(
            relay_dn.at[0], dn.at[unit_rows(left, 0, halfu), own_out],
            w_send.at[6], w_recv.at[6], d, right,
        ),
        remote(
            relay_dn.at[1], dn.at[unit_rows(right, halfu, halfu), own_out],
            w_send.at[7], w_recv.at[7], d, left,
        ),
    ]
    down_to_mate = remote(
        dn.at[:, own_out], dn.at[:, own_out], w_send.at[8], w_recv.at[8], mate, x
    )

    def chunk_rows(c):
        return pl.ds(pl.multiple_of(c * chunk, chunk), chunk)

    def block_rows(c, dy):
        return pl.ds(pl.multiple_of(c * chunk + dy * SLOTS, SLOTS), SLOTS)

    def spread(c):
        zz = lax.rem(z + offset(c) + nz, nz)
        row = lax.broadcasted_iota(jnp.int32, (chunk, experts), 0)
        dest = zz * ny + ((y + (row // SLOTS)) % ny)
        return jnp.where(
            lax.broadcasted_iota(jnp.int32, (chunk, experts), 1) == dest, 1.0, 0.0
        ).astype(bf16)

    def chosen(sel):
        slot = (lax.broadcasted_iota(jnp.int32, (chunk, tokens), 0) % SLOTS).astype(f32)
        return jnp.dot(sel, place_ref[...], preferred_element_type=f32) == slot

    def disp_copy(c, dy):
        zz = lax.rem(z + offset(c) + nz, nz)
        return remote(
            disp.at[block_rows(c, dy)], rows.at[x, block_rows(c, dy)],
            disp_send.at[c], disp_recv.at[c], dev(zz, lax.rem(y + dy, ny)), x,
        )

    def dispatch(c):
        pick = jnp.where(chosen(spread(c)), 1.0, 0.0).astype(bf16)
        block = jnp.dot(pick, tok_ref[...], preferred_element_type=f32).astype(bf16)
        disp[chunk_rows(c), :] = block
        for dy in range(1, ny):
            disp_copy(c, dy).start()

        @pl.when(c < nz - 1)
        def _():
            disp_copy(c, 0).start()

        @pl.when(c == nz - 1)
        def _():
            rows[x, block_rows(c, 0), :] = block[:SLOTS, :]

    ahead = min(2, nz)
    lat_copy.start()
    dispatch(0)
    for copy in to_side:
        copy.start()
    for c in range(1, ahead):
        dispatch(c)
    for copy in to_mate:
        copy.start()

    def head(h, carry):
        scores = jnp.dot(keys[...], query[h], preferred_element_type=f32) * score_scale + bias[...]
        lifted = jnp.exp(scores - jnp.max(scores, axis=0, keepdims=True))
        probs = (lifted / jnp.sum(lifted, axis=0, keepdims=True)).astype(bf16)
        attn[h] = lax.dot_general(
            probs, keys[:, :LAT], (((0,), (0,)), ((), ())), preferred_element_type=f32
        ).astype(bf16)
        return carry

    def first_half(c):
        return pl.ds(pl.multiple_of(c * chunk, chunk), half)

    def second_half(c):
        return pl.ds(pl.multiple_of(c * chunk + half, half), half)

    def x_copies(c):
        here = rows.at[x, chunk_rows(c)]
        return (
            remote(here, here, x_send.at[0, c], x_recv.at[0, c], d, right),
            remote(here, here, x_send.at[1, c], x_recv.at[1, c], d, left),
        )

    def x_relays(c):
        from_left, from_right = rows.at[left, first_half(c)], rows.at[right, second_half(c)]
        return (
            remote(from_left, from_left, x_send.at[2, c], x_recv.at[2, c], d, right),
            remote(from_right, from_right, x_send.at[3, c], x_recv.at[3, c], d, left),
        )

    def h_copies(c):
        here = hid.at[chunk_rows(c), unit_cols(x)]
        return (
            remote(here, here, h_send.at[0, c], h_recv.at[0, c], d, right),
            remote(here, here, h_send.at[1, c], h_recv.at[1, c], d, left),
        )

    def h_relays(c):
        from_left = hid.at[first_half(c), unit_cols(left)]
        from_right = hid.at[second_half(c), unit_cols(right)]
        return (
            remote(from_left, from_left, h_send.at[2, c], h_recv.at[2, c], d, right),
            remote(from_right, from_right, h_send.at[3, c], h_recv.at[3, c], d, left),
        )

    def ret_copy(c, dy):
        zz = lax.rem(z - offset(c) + nz, nz)
        return remote(
            outb.at[block_rows(c, dy)], ret.at[block_rows(c, dy)],
            ret_send.at[c], ret_recv.at[c], dev(zz, lax.rem(y - dy + ny, ny)), x,
        )

    def stage_arrive(c):
        @pl.when(c < nz - 1)
        def _():
            wait_in(rows.at[x, chunk_rows(c)], disp_recv.at[c])

        @pl.when(c == nz - 1)
        def _():
            wait_in(rows.at[x, pl.ds((nz - 1) * chunk, chunk - SLOTS)], disp_recv.at[c])

        for copy in x_copies(c):
            copy.start()

    def stage_relay(c):
        wait_in(rows.at[left, chunk_rows(c)], x_recv.at[0, c])
        wait_in(rows.at[right, chunk_rows(c)], x_recv.at[1, c])
        for copy in x_relays(c):
            copy.start()

    def stage_up(c):
        wait_in(rows.at[opposite, first_half(c)], x_recv.at[2, c])
        wait_in(rows.at[opposite, second_half(c)], x_recv.at[3, c])
        total = jnp.zeros((chunk, 2 * units), f32)
        for m in range(NX):
            total = total + jnp.dot(
                rows[m, chunk_rows(c), :], gu[m * width : (m + 1) * width, :],
                preferred_element_type=f32,
            )
        gate, upper = total[:, :units], total[:, units:]
        hid[chunk_rows(c), unit_cols(x)] = (gate / (1.0 + jnp.exp(-gate)) * upper).astype(bf16)
        for copy in h_copies(c):
            copy.start()

    def stage_hid(c):
        wait_in(hid.at[chunk_rows(c), unit_cols(left)], h_recv.at[0, c])
        wait_in(hid.at[chunk_rows(c), unit_cols(right)], h_recv.at[1, c])
        for copy in h_relays(c):
            copy.start()

    def stage_down(c):
        wait_in(hid.at[first_half(c), unit_cols(opposite)], h_recv.at[2, c])
        wait_in(hid.at[second_half(c), unit_cols(opposite)], h_recv.at[3, c])
        result = jnp.dot(hid[chunk_rows(c), :], dn[...], preferred_element_type=f32).astype(bf16)
        outb[chunk_rows(c), :] = result
        for dy in range(1, ny):
            ret_copy(c, dy).start()

        @pl.when(c < nz - 1)
        def _():
            ret_copy(c, 0).start()

        @pl.when(c == nz - 1)
        def _():
            ret[block_rows(c, 0), :] = result[:SLOTS, :]

    def stage_combine(c):
        @pl.when(c < nz - 1)
        def _():
            wait_in(ret.at[chunk_rows(c)], ret_recv.at[c])

        @pl.when(c == nz - 1)
        def _():
            wait_in(ret.at[pl.ds((nz - 1) * chunk + SLOTS, chunk - SLOTS)], ret_recv.at[c])

        sel = spread(c)
        taken = chosen(sel)
        back = ret[chunk_rows(c), :]
        total = acc[...]
        for part in (ghi_ref, glo_ref):
            scale = jnp.dot(sel, part[...], preferred_element_type=f32)
            scale = jnp.where(taken, scale, 0.0).astype(bf16)
            total = total + lax.dot_general(
                scale, back, (((0,), (0,)), ((), ())), preferred_element_type=f32
            )
        acc[...] = total

    acc[...] = jnp.zeros_like(acc)

    parts = min(4, nz)
    attn_copy = pltpu.make_async_copy(attn, attn_ref, q_sem.at[1])

    def step(t, carry):
        def at(delay, stage):
            @pl.when((t >= delay) & (t < delay + nz))
            def _():
                stage(t - delay)

        at(0, stage_arrive)

        @pl.when((t == 0) & (ahead < nz))
        def _():
            dispatch(ahead)

        @pl.when(t + ahead + 1 < nz)
        def _():
            dispatch(t + ahead + 1)

        at(2, stage_relay)

        @pl.when(t == 1)
        def _():
            wait_in(relay_dn.at[0], w_recv.at[4])
            wait_in(relay_dn.at[1], w_recv.at[5])
            for copy in relays:
                copy.start()

        @pl.when(t == 0)
        def _():
            local_query.wait()
            wait_in(keys.at[pl.ds(0, tokens)], lat_recv.at[0])

        @pl.when(t < parts)
        def _():
            lax.fori_loop(t * (heads // parts), (t + 1) * (heads // parts), head, 0)

        @pl.when(t == parts)
        def _():
            attn_copy.start()

        @pl.when(t == 3)
        def _():
            local_gate.wait()
            local_up.wait()
            wait_in(gu.at[mate_in, gate_cols], w_recv.at[0])
            wait_in(gu.at[mate_in, up_cols], w_recv.at[1])

        at(4, stage_hid)
        at(3, stage_up)

        @pl.when(t == 3)
        def _():
            local_down.wait()
            wait_in(dn.at[unit_rows(left, 0, units), own_out], w_recv.at[2])
            wait_in(dn.at[unit_rows(right, 0, units), own_out], w_recv.at[3])
            wait_in(dn.at[unit_rows(opposite, 0, halfu), own_out], w_recv.at[6])
            wait_in(dn.at[unit_rows(opposite, halfu, halfu), own_out], w_recv.at[7])
            down_to_mate.start()

        @pl.when(t == 5)
        def _():
            wait_in(dn.at[:, mate_out], w_recv.at[8])

        at(5, stage_down)
        at(7, stage_combine)
        return carry

    lax.fori_loop(0, nz + 7, step, 0)
    out_ref[...] = acc[...].astype(out_ref.dtype)

    attn_copy.wait()
    lat_copy.wait_send()
    for copy in to_side + to_mate + relays + [down_to_mate]:
        copy.wait_send()

    def drain(c, carry):
        for copy in x_copies(c) + x_relays(c) + h_copies(c) + h_relays(c):
            copy.wait_send()

        @pl.when(c < nz - 1)
        def _():
            wait_in(disp.at[chunk_rows(c)], disp_send.at[c])
            wait_in(outb.at[chunk_rows(c)], ret_send.at[c])

        @pl.when(c == nz - 1)
        def _():
            rest = pl.ds((nz - 1) * chunk + SLOTS, chunk - SLOTS)
            wait_in(disp.at[rest], disp_send.at[c])
            wait_in(outb.at[rest], ret_send.at[c])

        return carry

    lax.fori_loop(0, nz, drain, 0)


def layer(nz, ny, ids, scores, tok, gate, up, down, query, latent, docs):
    tokens, width = tok.shape
    units = gate.shape[1]
    piece = down.shape[1] // NX
    experts = nz * ny
    count = experts * SLOTS
    heads, feats, _ = query.shape
    vmem = pl.BlockSpec(memory_space=pltpu.VMEM)
    away = pl.BlockSpec(memory_space=pl.ANY)
    bf16 = jnp.bfloat16
    dma = pltpu.SemaphoreType.DMA
    return pl.pallas_call(
        functools.partial(layer_kernel, nz, ny),
        out_shape=(
            jax.ShapeDtypeStruct((tokens, width), bf16),
            jax.ShapeDtypeStruct((heads, tokens, LAT), bf16),
        ),
        in_specs=[vmem, vmem, vmem, away, away, away, away, vmem, vmem],
        out_specs=(vmem, away),
        scratch_shapes=[
            pltpu.VMEM((count, width), bf16),
            pltpu.VMEM((NX, count, width), bf16),
            pltpu.VMEM((NX * width, 2 * units), bf16),
            pltpu.VMEM((NX * units, width), bf16),
            pltpu.VMEM((2, units // 2, piece), bf16),
            pltpu.VMEM((count, NX * units), bf16),
            pltpu.VMEM((count, width), bf16),
            pltpu.VMEM((count, width), bf16),
            pltpu.VMEM((tokens, width), jnp.float32),
            pltpu.VMEM((experts, tokens), bf16),
            pltpu.VMEM((experts, tokens), bf16),
            pltpu.VMEM((experts, tokens), bf16),
            pltpu.VMEM((heads, feats, tokens), bf16),
            pltpu.VMEM((heads, tokens, LAT), bf16),
            pltpu.VMEM((2 * tokens, feats), bf16),
            pltpu.VMEM((2 * tokens, tokens), jnp.float32),
            dma((3,)),
            dma((2,)),
            dma((1,)),
            dma((1,)),
            dma((9,)),
            dma((9,)),
            dma((nz,)),
            dma((nz,)),
            dma((4, nz)),
            dma((4, nz)),
            dma((4, nz)),
            dma((4, nz)),
            dma((nz,)),
            dma((nz,)),
        ],
        compiler_params=pltpu.CompilerParams(
            collective_id=0, has_side_effects=True, vmem_limit_bytes=58 * 1024 * 1024
        ),
        name="layer",
    )(ids, scores, tok, gate, up, down, query, latent, docs)


def shards(
    queries,
    latents,
    doc_ids,
    hidden_rows,
    expert_ids,
    gate_scores,
    gate_weight,
    up_weight,
    down_weight,
):
    length = lax.axis_size("dp")
    moe_out, heads_out = layer(
        length // (2 * NY),
        NY,
        expert_ids.T,
        gate_scores.T,
        hidden_rows,
        gate_weight[0],
        up_weight[0],
        down_weight[0],
        queries.transpose(1, 2, 0),
        latents.T,
        doc_ids.reshape(length, -1),
    )
    return (heads_out.transpose(1, 0, 2), moe_out)


def solution(mesh):
    placed = (
        P("dp", "mp", None),
        P("dp", None),
        P(),
        P("dp", "mp"),
        P("dp", None),
        P("dp", None),
        P("dp", None, "mp"),
        P("dp", None, "mp"),
        P("dp", "mp", None),
    )
    return jax.shard_map(
        shards,
        mesh=mesh,
        in_specs=placed,
        out_specs=(P("dp", "mp", None), P("dp", "mp")),
        check_vma=False,
    )
```

time: 712 us -> 197 us (0.28)
  the two profiles are of different devices: /device:TPU:16 before, /device:TPU:40 now
where the time goes in v1:
time: 197 us
  Pallas kernels  192 us (97%)
  local copies, waits for them, and re-layouts  4.85 us (2%)
    pallas_call x1, Pallas kernels, layer(): pl.pallas_call(functools.partial(layer_kernel, nz, ny), out_shape=(jax.Sh...  192 us
    unnamed x4, local copies, waits for them, and re-layouts  4.85 us

profile of v1, /device:TPU:40, one launch (start us, length us, event | category | flops | bytes accessed | tf_op | source)
XLA Modules:
  0.0 197.2 jit_solution(9652554480270026165)
XLA Ops:
  0.6 191.7 %layer.1 = (bf16[128,1280]{1,0:T(8,128)(2,1)}, bf16[16,128,512]{2,1,0:T(8,128)(2,1)}) custom-call(s32[6,128]{1,0:T(8,128)} %bitcast.16, f32[6,128]{1,0:T(8,128)} %bitcast.17, bf16[128,1280]{1,0:T(8,128)(2,1)} %tok_ref.1, bf16[2560,384]{1,0:T(8,128)(2,1)} %bitcast.11, bf16[2560,384]{1,0:T(8,128)(2,1)} %bitcast.12, bf16[384,2560]{1,0:T(8,128)(2,1)} %bitcast.13, ...), custom_call_target="tpu_custom_call" | custom-call | tf_op jit(solution)/shard_map/layer/pallas_call | solution.py:512
  192.4 0.0 copy-start
  192.4 4.1 %copy.11 = bf16[128,16,512]{2,1,0:T(8,128)(2,1)} copy(bf16[128,16,512]{2,0,1:T(8,128)(2,1)} %bitcast.10) | data formatting | bytes 4194304
  196.5 0.0 copy-done
  196.5 0.7 copy.13
Async XLA Ops:
  192.4 4.1 %copy-start = (bf16[128,1280]{1,0:T(8,128)(2,1)S(1)}, bf16[128,1280]{1,0:T(8,128)(2,1)}, u32[]{:S(2)}) copy-start(bf16[128,1280]{1,0:T(8,128)(2,1)} %get-tuple-element.11) | copy-start | bytes 983044

commit v2 on v1

--- a/solution.py
+++ b/solution.py
@@ -9,10 +9,11 @@
 from jax.sharding import PartitionSpec as P
 
 LAT = 512
+LANES = 128
 SLOTS = 32
 NX = 4
 NY = 4
-Z_ORDER = {8: (1, -2, 2, -3, 3, 4, -1, 0), 4: (1, 2, -1, 0), 2: (1, 0)}
+Z_ORDER = {8: (-2, 3, -3, 4, 2, 1, -1, 0), 4: (1, 2, -1, 0), 2: (1, 0)}
 
 score_scale = 1.0 / math.sqrt(192.0)
 neg_large = -1e30
@@ -46,6 +47,7 @@
     ghi_ref,
     glo_ref,
     query,
+    wide,
     attn,
     keys,
     bias,
@@ -185,8 +187,6 @@
     bias[:tokens, :] = jnp.where(old_col == ids_row, 0.0, neg_large)
     bias[tokens:, :] = jnp.where((own_col == ids_row) & (row_at <= col_at), 0.0, neg_large)
 
-    pl.semaphore_wait(barrier, experts - 1 + 4)
-
     to_mate = [
         remote(gate_ref, gu.at[own_in, gate_cols], w_send.at[0], w_recv.at[0], mate, x),
         remote(up_ref, gu.at[own_in, up_cols], w_send.at[1], w_recv.at[1], mate, x),
@@ -249,10 +249,12 @@
             disp_send.at[c], disp_recv.at[c], dev(zz, lax.rem(y + dy, ny)), x,
         )
 
-    def dispatch(c):
+    def build(c):
         pick = jnp.where(chosen(spread(c)), 1.0, 0.0).astype(bf16)
         block = jnp.dot(pick, tok_ref[...], preferred_element_type=f32).astype(bf16)
         disp[chunk_rows(c), :] = block
+
+    def dispatch(c):
         for dy in range(1, ny):
             disp_copy(c, dy).start()
 
@@ -262,25 +264,30 @@
 
         @pl.when(c == nz - 1)
         def _():
-            rows[x, block_rows(c, 0), :] = block[:SLOTS, :]
+            rows[x, block_rows(c, 0), :] = disp[block_rows(c, 0), :]
 
     ahead = min(2, nz)
-    lat_copy.start()
-    dispatch(0)
-    for copy in to_side:
+    for c in range(ahead):
+        build(c)
+
+    pl.semaphore_wait(barrier, experts - 1 + 4)
+
+    for copy in to_side[:2]:
         copy.start()
-    for c in range(1, ahead):
+    for c in range(ahead):
         dispatch(c)
-    for copy in to_mate:
+    for copy in to_side[2:] + [lat_copy] + to_mate:
         copy.start()
 
     def head(h, carry):
         scores = jnp.dot(keys[...], query[h], preferred_element_type=f32) * score_scale + bias[...]
         lifted = jnp.exp(scores - jnp.max(scores, axis=0, keepdims=True))
         probs = (lifted / jnp.sum(lifted, axis=0, keepdims=True)).astype(bf16)
-        attn[h] = lax.dot_general(
+        value = lax.dot_general(
             probs, keys[:, :LAT], (((0,), (0,)), ((), ())), preferred_element_type=f32
-        ).astype(bf16)
+        )
+        for k in range(LAT // LANES):
+            wide[k, pl.ds(h, tokens, stride=heads), :] = value[:, k * LANES : (k + 1) * LANES]
         return carry
 
     def first_half(c):
@@ -406,22 +413,23 @@
     attn_copy = pltpu.make_async_copy(attn, attn_ref, q_sem.at[1])
 
     def step(t, carry):
-        def at(delay, stage):
-            @pl.when((t >= delay) & (t < delay + nz))
+        def at(delay, stage, count=nz):
+            @pl.when((t >= delay) & (t < delay + count))
             def _():
                 stage(t - delay)
 
+        at(1, stage_relay)
         at(0, stage_arrive)
 
         @pl.when((t == 0) & (ahead < nz))
         def _():
+            build(ahead)
             dispatch(ahead)
 
         @pl.when(t + ahead + 1 < nz)
         def _():
+            build(t + ahead + 1)
             dispatch(t + ahead + 1)
-
-        at(2, stage_relay)
 
         @pl.when(t == 1)
         def _():
@@ -441,19 +449,27 @@
 
         @pl.when(t == parts)
         def _():
+            def narrow(i, carry):
+                some = pl.ds(pl.multiple_of(i * tokens, tokens), tokens)
+                for k in range(LAT // LANES):
+                    attn[some, k * LANES : (k + 1) * LANES] = wide[k, some, :].astype(bf16)
+                return carry
+
+            lax.fori_loop(0, heads, narrow, 0)
             attn_copy.start()
 
-        @pl.when(t == 3)
+        at(2, stage_hid)
+
+        @pl.when(t == 1)
         def _():
             local_gate.wait()
             local_up.wait()
             wait_in(gu.at[mate_in, gate_cols], w_recv.at[0])
             wait_in(gu.at[mate_in, up_cols], w_recv.at[1])
 
-        at(4, stage_hid)
-        at(3, stage_up)
-
-        @pl.when(t == 3)
+        at(1, stage_up)
+
+        @pl.when(t == 2)
         def _():
             local_down.wait()
             wait_in(dn.at[unit_rows(left, 0, units), own_out], w_recv.at[2])
@@ -462,15 +478,22 @@
             wait_in(dn.at[unit_rows(opposite, halfu, halfu), own_out], w_recv.at[7])
             down_to_mate.start()
 
-        @pl.when(t == 5)
+        @pl.when(t == 3)
         def _():
             wait_in(dn.at[:, mate_out], w_recv.at[8])
 
-        at(5, stage_down)
-        at(7, stage_combine)
+        at(3, stage_down)
+        at(6, stage_combine, early)
         return carry
 
-    lax.fori_loop(0, nz + 7, step, 0)
+    early = min(3, nz - 1)
+    lax.fori_loop(0, nz + 3, step, 0)
+
+    def finish(c, carry):
+        stage_combine(c)
+        return carry
+
+    lax.fori_loop(early, nz, finish, 0)
     out_ref[...] = acc[...].astype(out_ref.dtype)
 
     attn_copy.wait()
@@ -513,7 +536,7 @@
         functools.partial(layer_kernel, nz, ny),
         out_shape=(
             jax.ShapeDtypeStruct((tokens, width), bf16),
-            jax.ShapeDtypeStruct((heads, tokens, LAT), bf16),
+            jax.ShapeDtypeStruct((tokens * heads, LAT), bf16),
         ),
         in_specs=[vmem, vmem, vmem, away, away, away, away, vmem, vmem],
         out_specs=(vmem, away),
@@ -531,7 +554,8 @@
             pltpu.VMEM((experts, tokens), bf16),
             pltpu.VMEM((experts, tokens), bf16),
             pltpu.VMEM((heads, feats, tokens), bf16),
-            pltpu.VMEM((heads, tokens, LAT), bf16),
+            pltpu.VMEM((LAT // LANES, tokens * heads, LANES), jnp.float32),
+            pltpu.VMEM((tokens * heads, LAT), bf16),
             pltpu.VMEM((2 * tokens, feats), bf16),
             pltpu.VMEM((2 * tokens, tokens), jnp.float32),
             dma((3,)),
@@ -568,7 +592,7 @@
     down_weight,
 ):
     length = lax.axis_size("dp")
-    moe_out, heads_out = layer(
+    moe_out, attn_out = layer(
         length // (2 * NY),
         NY,
         expert_ids.T,
@@ -581,7 +605,7 @@
         latents.T,
         doc_ids.reshape(length, -1),
     )
-    return (heads_out.transpose(1, 0, 2), moe_out)
+    return (attn_out.reshape(queries.shape[:2] + (LAT,)), moe_out)
 
 
 def solution(mesh):

time: 197 us -> 168 us (0.85)
  the two profiles are of different devices: /device:TPU:40 before, /device:TPU:16 now
where the time goes in v2:
time: 168 us; the launch traced here: 166 us
  Pallas kernels  161 us (96%)
  local copies, waits for them, and re-layouts  3.85 us (2%)
    pallas_call x1, Pallas kernels, layer(): pl.pallas_call(functools.partial(layer_kernel, nz, ny), out_shape=(jax.Sh...  161 us
    unnamed x4, local copies, waits for them, and re-layouts  3.85 us

profile of v2, /device:TPU:16, one launch (start us, length us, event | category | flops | bytes accessed | tf_op | source)
XLA Modules:
  0.0 165.9 jit_solution(5347534795871731558)
XLA Ops:
  0.6 161.4 %layer.1 = (bf16[128,1280]{1,0:T(8,128)(2,1)}, bf16[2048,512]{1,0:T(8,128)(2,1)}) custom-call(s32[6,128]{1,0:T(8,128)} %bitcast.16, f32[6,128]{1,0:T(8,128)} %bitcast.17, bf16[128,1280]{1,0:T(8,128)(2,1)} %tok_ref.1, bf16[2560,384]{1,0:T(8,128)(2,1)} %bitcast.11, bf16[2560,384]{1,0:T(8,128)(2,1)} %bitcast.12, bf16[384,2560]{1,0:T(8,128)(2,1)} %bitcast.13, ...), custom_call_target="tpu_custom_call" | custom-call | tf_op jit(solution)/shard_map/layer/pallas_call | solution.py:535
  162.0 0.0 copy-start
  162.1 3.1 %copy.13 = bf16[128,16,512]{2,1,0:T(8,128)(2,1)} copy(bf16[128,16,512]{2,1,0:T(8,128)(2,1)} %bitcast.10) | data formatting | bytes 4194304
  165.2 0.0 copy-done
  165.2 0.7 copy.14
Async XLA Ops:
  162.0 3.1 %copy-start = (bf16[128,1280]{1,0:T(8,128)(2,1)S(1)}, bf16[128,1280]{1,0:T(8,128)(2,1)}, u32[]{:S(2)}) copy-start(bf16[128,1280]{1,0:T(8,128)(2,1)} %get-tuple-element.9) | copy-start | bytes 983044

commit v3 on v2

--- a/solution.py
+++ b/solution.py
@@ -11,9 +11,11 @@
 LAT = 512
 LANES = 128
 SLOTS = 32
+CAP = 30
+CHUNK = 64
 NX = 4
 NY = 4
-Z_ORDER = {8: (-2, 3, -3, 4, 2, 1, -1, 0), 4: (1, 2, -1, 0), 2: (1, 0)}
+Z_ORDER = {8: (0, -2, 4, 3, -3, 2, 1, -1), 4: (0, 2, 1, -1), 2: (0, 1)}
 
 score_scale = 1.0 / math.sqrt(192.0)
 neg_large = -1e30
@@ -35,6 +37,7 @@
     out_ref,
     attn_ref,
     disp,
+    land,
     rows,
     gu,
     dn,
@@ -72,8 +75,11 @@
     half_in, units = gate_ref.shape
     piece = down_ref.shape[1] // NX
     experts = nz * ny
-    chunk = ny * SLOTS
-    half = chunk // 2
+    plane = ny * SLOTS
+    chunk, half = CHUNK, CHUNK // 2
+    per = CHUNK // SLOTS
+    sent, packed = experts * SLOTS // chunk, experts * CAP // chunk
+    own_chunk = Z_ORDER[nz].index(0) * (plane // chunk)
     f32, bf16 = jnp.float32, jnp.bfloat16
 
     d = lax.axis_index("dp")
@@ -227,68 +233,74 @@
     def chunk_rows(c):
         return pl.ds(pl.multiple_of(c * chunk, chunk), chunk)
 
-    def block_rows(c, dy):
-        return pl.ds(pl.multiple_of(c * chunk + dy * SLOTS, SLOTS), SLOTS)
-
-    def spread(c):
-        zz = lax.rem(z + offset(c) + nz, nz)
-        row = lax.broadcasted_iota(jnp.int32, (chunk, experts), 0)
-        dest = zz * ny + ((y + (row // SLOTS)) % ny)
+    def block_rows(b):
+        return pl.ds(pl.multiple_of(b * SLOTS, SLOTS), SLOTS)
+
+    def peer(b, way):
+        zz = lax.rem(z + way * offset(lax.div(b, ny)) + nz, nz)
+        return dev(zz, lax.rem(y + way * lax.rem(b, ny) + ny, ny))
+
+    def spread(at, first, count):
+        zz = lax.rem(z + offset(at) + nz, nz)
+        row = lax.broadcasted_iota(jnp.int32, (count, experts), 0)
+        dest = zz * ny + ((y + first + (row // SLOTS)) % ny)
         return jnp.where(
-            lax.broadcasted_iota(jnp.int32, (chunk, experts), 1) == dest, 1.0, 0.0
+            lax.broadcasted_iota(jnp.int32, (count, experts), 1) == dest, 1.0, 0.0
         ).astype(bf16)
 
     def chosen(sel):
-        slot = (lax.broadcasted_iota(jnp.int32, (chunk, tokens), 0) % SLOTS).astype(f32)
+        count = sel.shape[0]
+        slot = (lax.broadcasted_iota(jnp.int32, (count, tokens), 0) % SLOTS).astype(f32)
         return jnp.dot(sel, place_ref[...], preferred_element_type=f32) == slot
 
-    def disp_copy(c, dy):
-        zz = lax.rem(z + offset(c) + nz, nz)
-        return remote(
-            disp.at[block_rows(c, dy)], rows.at[x, block_rows(c, dy)],
-            disp_send.at[c], disp_recv.at[c], dev(zz, lax.rem(y + dy, ny)), x,
-        )
-
     def build(c):
-        pick = jnp.where(chosen(spread(c)), 1.0, 0.0).astype(bf16)
+        first = c * per
+        sel = spread(lax.div(first, ny), lax.rem(first, ny), chunk)
+        pick = jnp.where(chosen(sel), 1.0, 0.0).astype(bf16)
         block = jnp.dot(pick, tok_ref[...], preferred_element_type=f32).astype(bf16)
         disp[chunk_rows(c), :] = block
 
+    def disp_copy(c, i):
+        b = c * per + i
+        return remote(
+            disp.at[block_rows(b)], land.at[block_rows(b)],
+            disp_send.at[c], disp_recv.at[c], peer(b, 1), x,
+        )
+
+    def own_block(c):
+        return pl.ds(pl.multiple_of(c * chunk, chunk), SLOTS)
+
+    def other_blocks(c):
+        return pl.ds(pl.multiple_of(c * chunk + SLOTS, SLOTS), chunk - SLOTS)
+
+    def per_chunk(c, yes, no):
+        pl.when(c == own_chunk)(yes)
+        pl.when(c != own_chunk)(no)
+
     def dispatch(c):
-        for dy in range(1, ny):
-            disp_copy(c, dy).start()
-
-        @pl.when(c < nz - 1)
-        def _():
-            disp_copy(c, 0).start()
-
-        @pl.when(c == nz - 1)
-        def _():
-            rows[x, block_rows(c, 0), :] = disp[block_rows(c, 0), :]
-
-    ahead = min(2, nz)
-    for c in range(ahead):
-        build(c)
+        for i in range(1, per):
+            disp_copy(c, i).start()
+
+        def keep():
+            land[own_block(c), :] = disp[own_block(c), :]
+
+        per_chunk(c, keep, lambda: disp_copy(c, 0).start())
+
+    ahead = min(6, sent)
+    for c in range(2):
+        build(jnp.int32(c))
 
     pl.semaphore_wait(barrier, experts - 1 + 4)
 
     for copy in to_side[:2]:
         copy.start()
     for c in range(ahead):
-        dispatch(c)
-    for copy in to_side[2:] + [lat_copy] + to_mate:
-        copy.start()
-
-    def head(h, carry):
-        scores = jnp.dot(keys[...], query[h], preferred_element_type=f32) * score_scale + bias[...]
-        lifted = jnp.exp(scores - jnp.max(scores, axis=0, keepdims=True))
-        probs = (lifted / jnp.sum(lifted, axis=0, keepdims=True)).astype(bf16)
-        value = lax.dot_general(
-            probs, keys[:, :LAT], (((0,), (0,)), ((), ())), preferred_element_type=f32
-        )
-        for k in range(LAT // LANES):
-            wide[k, pl.ds(h, tokens, stride=heads), :] = value[:, k * LANES : (k + 1) * LANES]
-        return carry
+        if c >= 2:
+            build(jnp.int32(c))
+        dispatch(jnp.int32(c))
+        if c == 1:
+            for copy in to_side[2:] + [lat_copy] + to_mate:
+                copy.start()
 
     def first_half(c):
         return pl.ds(pl.multiple_of(c * chunk, chunk), half)
@@ -311,36 +323,47 @@
         )
 
     def h_copies(c):
-        here = hid.at[chunk_rows(c), unit_cols(x)]
+        here = hid.at[chunk_rows(c + 1), unit_cols(x)]
         return (
             remote(here, here, h_send.at[0, c], h_recv.at[0, c], d, right),
             remote(here, here, h_send.at[1, c], h_recv.at[1, c], d, left),
         )
 
     def h_relays(c):
-        from_left = hid.at[first_half(c), unit_cols(left)]
-        from_right = hid.at[second_half(c), unit_cols(right)]
+        from_left = hid.at[first_half(c + 1), unit_cols(left)]
+        from_right = hid.at[second_half(c + 1), unit_cols(right)]
         return (
             remote(from_left, from_left, h_send.at[2, c], h_recv.at[2, c], d, right),
             remote(from_right, from_right, h_send.at[3, c], h_recv.at[3, c], d, left),
         )
 
-    def ret_copy(c, dy):
-        zz = lax.rem(z - offset(c) + nz, nz)
+    def ret_copy(c, i):
+        b = c * per + i
         return remote(
-            outb.at[block_rows(c, dy)], ret.at[block_rows(c, dy)],
-            ret_send.at[c], ret_recv.at[c], dev(zz, lax.rem(y - dy + ny, ny)), x,
-        )
-
-    def stage_arrive(c):
-        @pl.when(c < nz - 1)
-        def _():
-            wait_in(rows.at[x, chunk_rows(c)], disp_recv.at[c])
-
-        @pl.when(c == nz - 1)
-        def _():
-            wait_in(rows.at[x, pl.ds((nz - 1) * chunk, chunk - SLOTS)], disp_recv.at[c])
-
+            outb.at[block_rows(b)], ret.at[block_rows(b)],
+            ret_send.at[c], ret_recv.at[c], peer(b, -1), x,
+        )
+
+    def arrived(c):
+        per_chunk(
+            c,
+            lambda: wait_in(land.at[other_blocks(c)], disp_recv.at[c]),
+            lambda: wait_in(land.at[chunk_rows(c)], disp_recv.at[c]),
+        )
+
+    def stage_pack(c):
+        @pl.when(c == 0)
+        def _():
+            arrived(c)
+
+        arrived(c + 1)
+        row = lax.broadcasted_iota(jnp.int32, (chunk, 2 * chunk), 0)
+        col = lax.broadcasted_iota(jnp.int32, (chunk, 2 * chunk), 1)
+        take = col == row + (SLOTS - CAP) * ((row + c * chunk) // CAP)
+        window = land[pl.ds(pl.multiple_of(c * chunk, chunk), 2 * chunk), :]
+        rows[x, chunk_rows(c), :] = jnp.dot(
+            jnp.where(take, 1.0, 0.0).astype(bf16), window, preferred_element_type=f32
+        ).astype(bf16)
         for copy in x_copies(c):
             copy.start()
 
@@ -360,44 +383,50 @@
                 preferred_element_type=f32,
             )
         gate, upper = total[:, :units], total[:, units:]
-        hid[chunk_rows(c), unit_cols(x)] = (gate / (1.0 + jnp.exp(-gate)) * upper).astype(bf16)
+        hid[chunk_rows(c + 1), unit_cols(x)] = (gate / (1.0 + jnp.exp(-gate)) * upper).astype(bf16)
         for copy in h_copies(c):
             copy.start()
 
     def stage_hid(c):
-        wait_in(hid.at[chunk_rows(c), unit_cols(left)], h_recv.at[0, c])
-        wait_in(hid.at[chunk_rows(c), unit_cols(right)], h_recv.at[1, c])
+        wait_in(hid.at[chunk_rows(c + 1), unit_cols(left)], h_recv.at[0, c])
+        wait_in(hid.at[chunk_rows(c + 1), unit_cols(right)], h_recv.at[1, c])
         for copy in h_relays(c):
             copy.start()
 
     def stage_down(c):
-        wait_in(hid.at[first_half(c), unit_cols(opposite)], h_recv.at[2, c])
-        wait_in(hid.at[second_half(c), unit_cols(opposite)], h_recv.at[3, c])
-        result = jnp.dot(hid[chunk_rows(c), :], dn[...], preferred_element_type=f32).astype(bf16)
-        outb[chunk_rows(c), :] = result
-        for dy in range(1, ny):
-            ret_copy(c, dy).start()
-
-        @pl.when(c < nz - 1)
-        def _():
-            ret_copy(c, 0).start()
-
-        @pl.when(c == nz - 1)
-        def _():
-            ret[block_rows(c, 0), :] = result[:SLOTS, :]
-
-    def stage_combine(c):
-        @pl.when(c < nz - 1)
-        def _():
-            wait_in(ret.at[chunk_rows(c)], ret_recv.at[c])
-
-        @pl.when(c == nz - 1)
-        def _():
-            wait_in(ret.at[pl.ds((nz - 1) * chunk + SLOTS, chunk - SLOTS)], ret_recv.at[c])
-
-        sel = spread(c)
+        @pl.when(c < packed)
+        def _():
+            wait_in(hid.at[first_half(c + 1), unit_cols(opposite)], h_recv.at[2, c])
+            wait_in(hid.at[second_half(c + 1), unit_cols(opposite)], h_recv.at[3, c])
+
+        row = lax.broadcasted_iota(jnp.int32, (chunk, 2 * chunk), 0)
+        col = lax.broadcasted_iota(jnp.int32, (chunk, 2 * chunk), 1)
+        place = c * chunk + row
+        take = (col + (c - 1) * chunk == place - (SLOTS - CAP) * (place // SLOTS)) & (row % SLOTS < CAP)
+        window = hid[pl.ds(pl.multiple_of(c * chunk, chunk), 2 * chunk), :]
+        value = jnp.dot(
+            jnp.where(take, 1.0, 0.0).astype(bf16), window, preferred_element_type=f32
+        ).astype(bf16)
+        outb[chunk_rows(c), :] = jnp.dot(value, dn[...], preferred_element_type=f32).astype(bf16)
+        for i in range(1, per):
+            ret_copy(c, i).start()
+
+        def keep():
+            ret[own_block(c), :] = outb[own_block(c), :]
+
+        per_chunk(c, keep, lambda: ret_copy(c, 0).start())
+
+    def stage_combine(at):
+        for i in range(plane // chunk):
+            c = at * (plane // chunk) + i
+            per_chunk(
+                c,
+                lambda c=c: wait_in(ret.at[other_blocks(c)], ret_recv.at[c]),
+                lambda c=c: wait_in(ret.at[chunk_rows(c)], ret_recv.at[c]),
+            )
+        sel = spread(at, 0, plane)
         taken = chosen(sel)
-        back = ret[chunk_rows(c), :]
+        back = ret[pl.ds(pl.multiple_of(at * plane, plane), plane), :]
         total = acc[...]
         for part in (ghi_ref, glo_ref):
             scale = jnp.dot(sel, part[...], preferred_element_type=f32)
@@ -407,31 +436,41 @@
             )
         acc[...] = total
 
+    hid[:chunk, :] = jnp.zeros((chunk, hid.shape[1]), bf16)
+    hid[(packed + 1) * chunk :, :] = jnp.zeros((chunk, hid.shape[1]), bf16)
     acc[...] = jnp.zeros_like(acc)
 
-    parts = min(4, nz)
+    def head(h, carry):
+        scores = jnp.dot(keys[...], query[h], preferred_element_type=f32) * score_scale + bias[...]
+        lifted = jnp.exp(scores - jnp.max(scores, axis=0, keepdims=True))
+        probs = (lifted / jnp.sum(lifted, axis=0, keepdims=True)).astype(bf16)
+        value = lax.dot_general(
+            probs, keys[:, :LAT], (((0,), (0,)), ((), ())), preferred_element_type=f32
+        )
+        for k in range(LAT // LANES):
+            wide[k, pl.ds(h, tokens, stride=heads), :] = value[:, k * LANES : (k + 1) * LANES]
+        return carry
+
+    parts = min(8, sent)
     attn_copy = pltpu.make_async_copy(attn, attn_ref, q_sem.at[1])
+    early = min(2, nz)
 
     def step(t, carry):
-        def at(delay, stage, count=nz):
+        def at(delay, stage, count):
             @pl.when((t >= delay) & (t < delay + count))
             def _():
                 stage(t - delay)
 
-        at(1, stage_relay)
-        at(0, stage_arrive)
-
-        @pl.when((t == 0) & (ahead < nz))
-        def _():
-            build(ahead)
-            dispatch(ahead)
-
-        @pl.when(t + ahead + 1 < nz)
-        def _():
-            build(t + ahead + 1)
-            dispatch(t + ahead + 1)
-
-        @pl.when(t == 1)
+        at(0, stage_pack, packed)
+
+        @pl.when(t + ahead < sent)
+        def _():
+            build(t + ahead)
+            dispatch(t + ahead)
+
+        at(1, stage_relay, packed)
+
+        @pl.when(t == 2)
         def _():
             wait_in(relay_dn.at[0], w_recv.at[4])
             wait_in(relay_dn.at[1], w_recv.at[5])
@@ -458,18 +497,17 @@
             lax.fori_loop(0, heads, narrow, 0)
             attn_copy.start()
 
-        at(2, stage_hid)
-
-        @pl.when(t == 1)
+        @pl.when(t == 2)
         def _():
             local_gate.wait()
             local_up.wait()
             wait_in(gu.at[mate_in, gate_cols], w_recv.at[0])
             wait_in(gu.at[mate_in, up_cols], w_recv.at[1])
 
-        at(1, stage_up)
-
-        @pl.when(t == 2)
+        at(2, stage_up, packed)
+        at(3, stage_hid, packed)
+
+        @pl.when(t == 3)
         def _():
             local_down.wait()
             wait_in(dn.at[unit_rows(left, 0, units), own_out], w_recv.at[2])
@@ -478,19 +516,24 @@
             wait_in(dn.at[unit_rows(opposite, halfu, halfu), own_out], w_recv.at[7])
             down_to_mate.start()
 
-        @pl.when(t == 3)
+        @pl.when(t == 4)
         def _():
             wait_in(dn.at[:, mate_out], w_recv.at[8])
 
-        at(3, stage_down)
-        at(6, stage_combine, early)
+        at(4, stage_down, sent)
+
+        @pl.when(lax.rem(t, 2) == 0)
+        def _():
+            @pl.when((t >= 14) & (t < 14 + 2 * early))
+            def _():
+                stage_combine(lax.div(t - 14, 2))
+
         return carry
 
-    early = min(3, nz - 1)
-    lax.fori_loop(0, nz + 3, step, 0)
-
-    def finish(c, carry):
-        stage_combine(c)
+    lax.fori_loop(0, sent + 4, step, 0)
+
+    def finish(at, carry):
+        stage_combine(at)
         return carry
 
     lax.fori_loop(early, nz, finish, 0)
@@ -504,21 +547,23 @@
     def drain(c, carry):
         for copy in x_copies(c) + x_relays(c) + h_copies(c) + h_relays(c):
             copy.wait_send()
-
-        @pl.when(c < nz - 1)
-        def _():
+        return carry
+
+    lax.fori_loop(0, packed, drain, 0)
+
+    def drain_sent(c, carry):
+        def some():
+            wait_in(disp.at[other_blocks(c)], disp_send.at[c])
+            wait_in(outb.at[other_blocks(c)], ret_send.at[c])
+
+        def whole():
             wait_in(disp.at[chunk_rows(c)], disp_send.at[c])
             wait_in(outb.at[chunk_rows(c)], ret_send.at[c])
 
-        @pl.when(c == nz - 1)
-        def _():
-            rest = pl.ds((nz - 1) * chunk + SLOTS, chunk - SLOTS)
-            wait_in(disp.at[rest], disp_send.at[c])
-            wait_in(outb.at[rest], ret_send.at[c])
-
+        per_chunk(c, some, whole)
         return carry
 
-    lax.fori_loop(0, nz, drain, 0)
+    lax.fori_loop(0, sent, drain_sent, 0)
 
 
 def layer(nz, ny, ids, scores, tok, gate, up, down, query, latent, docs):
@@ -526,7 +571,8 @@
     units = gate.shape[1]
     piece = down.shape[1] // NX
     experts = nz * ny
-    count = experts * SLOTS
+    count, packed = experts * SLOTS, experts * CAP
+    sent_n, packed_n = count // CHUNK, packed // CHUNK
     heads, feats, _ = query.shape
     vmem = pl.BlockSpec(memory_space=pltpu.VMEM)
     away = pl.BlockSpec(memory_space=pl.ANY)
@@ -542,11 +588,12 @@
         out_specs=(vmem, away),
         scratch_shapes=[
             pltpu.VMEM((count, width), bf16),
-            pltpu.VMEM((NX, count, width), bf16),
+            pltpu.VMEM((count, width), bf16),
+            pltpu.VMEM((NX, packed, width), bf16),
             pltpu.VMEM((NX * width, 2 * units), bf16),
             pltpu.VMEM((NX * units, width), bf16),
             pltpu.VMEM((2, units // 2, piece), bf16),
-            pltpu.VMEM((count, NX * units), bf16),
+            pltpu.VMEM((packed + 2 * CHUNK, NX * units), bf16),
             pltpu.VMEM((count, width), bf16),
             pltpu.VMEM((count, width), bf16),
             pltpu.VMEM((tokens, width), jnp.float32),
@@ -564,14 +611,14 @@
             dma((1,)),
             dma((9,)),
             dma((9,)),
-            dma((nz,)),
-            dma((nz,)),
-            dma((4, nz)),
-            dma((4, nz)),
-            dma((4, nz)),
-            dma((4, nz)),
-            dma((nz,)),
-            dma((nz,)),
+            dma((sent_n,)),
+            dma((sent_n,)),
+            dma((4, packed_n)),
+            dma((4, packed_n)),
+            dma((4, packed_n)),
+            dma((4, packed_n)),
+            dma((sent_n,)),
+            dma((sent_n,)),
         ],
         compiler_params=pltpu.CompilerParams(
             collective_id=0, has_side_effects=True, vmem_limit_bytes=58 * 1024 * 1024

time: 168 us -> 161 us (0.958); the launches traced: 166 us -> 161 us
  Pallas kernels: 161 us -> 156 us
    pallas_call x1, Pallas kernels: 161 us -> 156 us  [layer(): pl.pallas_call(functools.partial(layer_kernel, nz, ny), out_shape=(jax.Sh...]
where the time goes in v3:
time: 161 us
  Pallas kernels  156 us (97%)
  local copies, waits for them, and re-layouts  3.85 us (2%)
    pallas_call x1, Pallas kernels, layer(): pl.pallas_call(functools.partial(layer_kernel, nz, ny), out_shape=(jax.Sh...  156 us
    unnamed x4, local copies, waits for them, and re-layouts  3.85 us

profile of v3, /device:TPU:16, one launch (start us, length us, event | category | flops | bytes accessed | tf_op | source)
XLA Modules:
  0.0 160.7 jit_solution(7611408521679623625)
XLA Ops:
  0.6 156.2 %layer.1 = (bf16[128,1280]{1,0:T(8,128)(2,1)}, bf16[2048,512]{1,0:T(8,128)(2,1)}) custom-call(s32[6,128]{1,0:T(8,128)} %bitcast.16, f32[6,128]{1,0:T(8,128)} %bitcast.17, bf16[128,1280]{1,0:T(8,128)(2,1)} %tok_ref.1, bf16[2560,384]{1,0:T(8,128)(2,1)} %bitcast.11, bf16[2560,384]{1,0:T(8,128)(2,1)} %bitcast.12, bf16[384,2560]{1,0:T(8,128)(2,1)} %bitcast.13, ...), custom_call_target="tpu_custom_call" | custom-call | tf_op jit(solution)/shard_map/layer/pallas_call | solution.py:581
  156.8 0.0 copy-start
  156.8 3.1 %copy.13 = bf16[128,16,512]{2,1,0:T(8,128)(2,1)} copy(bf16[128,16,512]{2,1,0:T(8,128)(2,1)} %bitcast.10) | data formatting | bytes 4194304
  159.9 0.0 copy-done
  159.9 0.7 copy.14
Async XLA Ops:
  156.8 3.1 %copy-start = (bf16[128,1280]{1,0:T(8,128)(2,1)S(1)}, bf16[128,1280]{1,0:T(8,128)(2,1)}, u32[]{:S(2)}) copy-start(bf16[128,1280]{1,0:T(8,128)(2,1)} %get-tuple-element.9) | copy-start | bytes 983044

commit v4 on v3

v4 whole, which is shorter than its diff:
```python
import functools
import math

import jax
import jax.numpy as jnp
from jax import lax
from jax.experimental import pallas as pl
from jax.experimental.pallas import tpu as pltpu
from jax.sharding import PartitionSpec as P

LAT = 512
LANES = 128
SLOTS = 32
CHUNK = 64
NX = 4
NY = 4
PLANES = (2, -2, 3, -3, 4, 1, -1, 0)
FAR = 5
CHUNKS = (0, 1, 2, 3, 4, 5, 10, 11, 6, 7, 12, 13, 8, 9, 14, 15)
BACK = (0, 1, 2, 5, 3, 6, 4, 7)

score_scale = 1.0 / math.sqrt(192.0)
neg_large = -1e30
MESH = pl.DeviceIdType.MESH


def layer_kernel(
    nz,
    ny,
    ids_ref,
    score_ref,
    tok_ref,
    gate_ref,
    up_ref,
    down_ref,
    query_ref,
    latent_ref,
    doc_ref,
    out_ref,
    attn_ref,
    far_disp,
    near_disp,
    tok,
    wide_tok,
    rows,
    gu,
    dn,
    relay_dn,
    hid,
    outb,
    ret,
    acc,
    place_ref,
    ghi_ref,
    glo_ref,
    query,
    wide,
    attn,
    keys,
    bias,
    local_sem,
    q_sem,
    lat_send,
    lat_recv,
    w_send,
    w_recv,
    t_send,
    t_recv,
    f_send,
    f_recv,
    disp_send,
    disp_recv,
    x_send,
    x_recv,
    h_send,
    h_recv,
    ret_send,
    ret_recv,
):
    top, tokens = ids_ref.shape
    heads = query_ref.shape[0]
    width = tok_ref.shape[1]
    half_in, units = gate_ref.shape
    piece = down_ref.shape[1] // NX
    experts = nz * ny
    named_rows = LANES
    plane = ny * SLOTS
    chunk, half = CHUNK, CHUNK // 2
    per = CHUNK // SLOTS
    per_plane = plane // chunk
    chunks, far = nz * per_plane, FAR * per_plane
    own_chunk = PLANES.index(0) * per_plane
    f32, bf16 = jnp.float32, jnp.bfloat16

    d = lax.axis_index("dp")
    x = lax.axis_index("mp")
    s = lax.rem(d, 2)
    p = lax.div(d, 2)
    z = lax.div(p, ny)
    y = lax.rem(p, ny)
    right = lax.rem(x + 1, NX)
    left = lax.rem(x + NX - 1, NX)
    opposite = lax.rem(x + 2, NX)
    mate = d + 1 - 2 * s

    def dev(zz, yy):
        return (zz * ny + yy) * 2 + s

    def entry(table, i):
        total = 0
        for at, value in enumerate(table):
            total = total + jnp.where(i == at, value, 0)
        return total

    def offset(at):
        return entry(PLANES, at)

    def remote(src, dst, send, recv, dd, xx):
        return pltpu.make_async_remote_copy(
            src_ref=src, dst_ref=dst, send_sem=send, recv_sem=recv,
            device_id=(dd, xx), device_id_type=MESH,
        )

    def wait_in(ref, sem):
        pltpu.make_async_copy(ref, ref, sem).wait()

    own_in = pl.ds(pl.multiple_of(s * half_in, half_in), half_in)
    mate_in = pl.ds(pl.multiple_of((1 - s) * half_in, half_in), half_in)
    own_out = pl.ds(pl.multiple_of(s * piece, piece), piece)
    mate_out = pl.ds(pl.multiple_of((1 - s) * piece, piece), piece)
    gate_cols, up_cols = pl.ds(0, units), pl.ds(units, units)

    def unit_rows(q, start, count):
        return pl.ds(pl.multiple_of(q * units + start, units // 2), count)

    def unit_cols(q):
        return pl.ds(pl.multiple_of(q * units, units), units)

    def down_cols(q):
        return pl.ds(pl.multiple_of(q * piece, piece), piece)

    local_gate = pltpu.make_async_copy(gate_ref, gu.at[own_in, gate_cols], local_sem.at[0])
    local_up = pltpu.make_async_copy(up_ref, gu.at[own_in, up_cols], local_sem.at[1])
    local_down = pltpu.make_async_copy(
        down_ref.at[:, down_cols(x)], dn.at[unit_rows(x, 0, units), own_out], local_sem.at[2]
    )
    local_gate.start()
    local_up.start()
    local_down.start()
    local_query = pltpu.make_async_copy(query_ref, query, q_sem.at[0])
    local_query.start()

    barrier = pltpu.get_barrier_semaphore()

    def greet(dd, xx):
        pl.semaphore_signal(barrier, inc=1, device_id=(dd, xx), device_id_type=MESH)

    ring = experts * 2
    beside = lax.rem(d + 2 * s - 1 + ring, ring)
    following = lax.rem(d + 1, ring)
    greet(mate, x)
    greet(beside, x)
    greet(d, right)
    greet(d, left)

    def greet_peer(k, carry):
        greet(lax.rem(p + k, experts) * 2 + s, x)
        return carry

    lax.fori_loop(1, experts, greet_peer, 0)

    expert_at = lax.broadcasted_iota(jnp.int32, (named_rows, tokens), 0)
    named = jnp.zeros((named_rows, tokens), f32)
    weight = jnp.zeros((named_rows, tokens), f32)
    for k in range(top):
        hit = ids_ref[k : k + 1, :] == expert_at
        named = named + jnp.where(hit, 1.0, 0.0)
        weight = weight + jnp.where(hit, score_ref[k : k + 1, :], 0.0)
    row_at = lax.broadcasted_iota(jnp.int32, (tokens, tokens), 0)
    col_at = lax.broadcasted_iota(jnp.int32, (tokens, tokens), 1)
    before = jnp.dot(
        named.astype(bf16),
        jnp.where(row_at < col_at, 1.0, 0.0).astype(bf16),
        preferred_element_type=f32,
    )
    place_ref[...] = jnp.where(named > 0.5, before, -1.0).astype(bf16)
    whole = weight.astype(bf16)
    ghi_ref[...] = whole
    glo_ref[...] = (weight - whole.astype(f32)).astype(bf16)

    same = row_at == col_at
    unit = jnp.where(same, 1.0, 0.0).astype(bf16)
    keys[tokens:, :] = lax.dot_general(
        unit, latent_ref[...], (((1,), (1,)), ((), ())), preferred_element_type=f32
    ).astype(bf16)
    tok[0, :, :width] = tok_ref[...]
    tok[0, :, width:] = lax.dot_general(
        unit, place_ref[...], (((1,), (1,)), ((), ())), preferred_element_type=f32
    ).astype(bf16)
    lat_copy = remote(
        keys.at[pl.ds(tokens, tokens)], keys.at[pl.ds(0, tokens)],
        lat_send.at[0], lat_recv.at[0], following, x,
    )
    own_ids = doc_ref[pl.ds(d, 1), :]
    old_ids = doc_ref[pl.ds(lax.rem(d + ring - 1, ring), 1), :]
    own_col = jnp.sum(jnp.where(same, own_ids, 0).astype(f32), axis=1, keepdims=True)
    old_col = jnp.sum(jnp.where(same, old_ids, 0).astype(f32), axis=1, keepdims=True)
    old_col = old_col - jnp.where(d == 0, 1000.0, 0.0)
    ids_row = own_ids.astype(f32)
    bias[:tokens, :] = jnp.where(old_col == ids_row, 0.0, neg_large)
    bias[tokens:, :] = jnp.where((own_col == ids_row) & (row_at <= col_at), 0.0, neg_large)

    to_mate = [
        remote(gate_ref, gu.at[own_in, gate_cols], w_send.at[0], w_recv.at[0], mate, x),
        remote(up_ref, gu.at[own_in, up_cols], w_send.at[1], w_recv.at[1], mate, x),
    ]
    halfu = units // 2
    to_side = [
        remote(
            down_ref.at[:, down_cols(right)], dn.at[unit_rows(x, 0, units), own_out],
            w_send.at[2], w_recv.at[2], d, right,
        ),
        remote(
            down_ref.at[:, down_cols(left)], dn.at[unit_rows(x, 0, units), own_out],
            w_send.at[3], w_recv.at[3], d, left,
        ),
        remote(
            down_ref.at[pl.ds(0, halfu), down_cols(opposite)], relay_dn.at[0],
            w_send.at[4], w_recv.at[4], d, right,
        ),
        remote(
            down_ref.at[pl.ds(halfu, halfu), down_cols(opposite)], relay_dn.at[1],
            w_send.at[5], w_recv.at[5], d, left,
        ),
    ]
    relays = [
        remote(
            relay_dn.at[0], dn.at[unit_rows(left, 0, halfu), own_out],
            w_send.at[6], w_recv.at[6], d, right,
        ),
        remote(
            relay_dn.at[1], dn.at[unit_rows(right, halfu, halfu), own_out],
            w_send.at[7], w_recv.at[7], d, left,
        ),
    ]
    down_to_mate = remote(
        dn.at[:, own_out], dn.at[:, own_out], w_send.at[8], w_recv.at[8], mate, x
    )

    def chunk_rows(c):
        return pl.ds(pl.multiple_of(c * chunk, chunk), chunk)

    def block_rows(b):
        return pl.ds(pl.multiple_of(b * SLOTS, SLOTS), SLOTS)

    def chosen(plane_z, first, count, place, how):
        row = lax.broadcasted_iota(jnp.int32, (count, named_rows), 0)
        dest = plane_z * ny + ((y + first + (row // SLOTS)) % ny)
        sel = jnp.where(
            lax.broadcasted_iota(jnp.int32, (count, named_rows), 1) == dest, 1.0, 0.0
        ).astype(bf16)
        slot = (lax.broadcasted_iota(jnp.int32, (count, tokens), 0) % SLOTS).astype(f32)
        held = lax.dot_general(sel, place, (((1,), (how,)), ((), ())), preferred_element_type=f32)
        return sel, held == slot

    z_up, z_down = dev(lax.rem(z + 1, nz), y), dev(lax.rem(z + nz - 1, nz), y)
    middle = nz // 2
    upper, lower = pl.ds(0, tokens // 2), pl.ds(tokens // 2, tokens // 2)

    def t_ref(way, hop, part=False):
        ref = tok.at[hop if way == 0 else (nz - hop) % nz]
        return ref.at[upper if way == 0 else lower] if part else ref

    def t_copy(way, hop):
        part = hop == middle
        return remote(
            t_ref(way, hop - 1, part), t_ref(way, hop, part),
            t_send.at[way, hop - 1], t_recv.at[way, hop - 1], (z_up, z_down)[way], x,
        )

    def hand_on(hop):
        for way in range(2):
            wait_in(t_ref(way, hop, hop == middle), t_recv.at[way, hop - 1])
            if hop < middle:
                t_copy(way, hop + 1).start()

    f_own = [
        remote(tok_ref, wide_tok.at[0, NX - 2], f_send.at[0], f_recv.at[0], d, right),
        remote(tok_ref, wide_tok.at[0, 0], f_send.at[1], f_recv.at[1], d, left),
    ]
    f_relays = [
        remote(
            wide_tok.at[0, NX - 2, upper], wide_tok.at[0, 1, upper],
            f_send.at[2], f_recv.at[2], d, right,
        ),
        remote(
            wide_tok.at[0, 0, lower], wide_tok.at[0, 1, lower],
            f_send.at[3], f_recv.at[3], d, left,
        ),
    ]
    f_planes = [
        remote(wide_tok.at[0], wide_tok.at[1], f_send.at[4], f_recv.at[4], z_up, x),
        remote(wide_tok.at[0], wide_tok.at[2], f_send.at[5], f_recv.at[5], z_down, x),
    ]

    def near_rows(c):
        return pl.ds(pl.multiple_of((c - far) * chunk, chunk), chunk)

    def near_block(b):
        return pl.ds(pl.multiple_of((b - far * per) * SLOTS, SLOTS), SLOTS)

    def build(c):
        at = lax.div(c, per_plane)
        source = lax.rem(offset(at) + nz, nz)
        _, hit = chosen(z, lax.rem(c, per_plane) * per, chunk, tok[source, :, width:], 1)
        pick = jnp.where(hit, 1.0, 0.0).astype(bf16)
        far_disp[chunk_rows(c), :] = jnp.dot(
            pick, tok[source, :, :width], preferred_element_type=f32
        ).astype(bf16)

        @pl.when(c >= far)
        def _():
            which = lax.rem(at - FAR + 1, nz - FAR)
            for j in range(NX - 1):
                near_disp[j, near_rows(c), :] = jnp.dot(
                    pick, wide_tok[which, j], preferred_element_type=f32
                ).astype(bf16)

    def disp_copy(b):
        c = lax.div(b, per)
        return remote(
            far_disp.at[block_rows(b)], rows.at[0, block_rows(b)],
            disp_send.at[c], disp_recv.at[c], dev(z, lax.rem(y + lax.rem(b, ny), ny)), x,
        )

    def near_copy(b):
        c = lax.div(b, per)
        return remote(
            near_disp.at[:, near_block(b)], rows.at[pl.ds(1, NX - 1), block_rows(b)],
            disp_send.at[c], disp_recv.at[c], dev(z, lax.rem(y + lax.rem(b, ny), ny)), x,
        )

    def dispatch(c):
        build(c)
        for i in range(per):
            b = c * per + i

            def send(b=b):
                disp_copy(b).start()

                @pl.when(c >= far)
                def _():
                    near_copy(b).start()

            def keep(b=b):
                rows[0, block_rows(b), :] = far_disp[block_rows(b), :]

                @pl.when(c >= far)
                def _():
                    for j in range(NX - 1):
                        rows[1 + j, block_rows(b), :] = near_disp[j, near_block(b), :]

            if i == 0:
                pl.when(lax.rem(c, per_plane) == 0)(keep)
                pl.when(lax.rem(c, per_plane) != 0)(send)
            else:
                send()

    def moved(c, sem):
        first = lax.rem(c, per_plane) == 0

        @pl.when((c < far) & first)
        def _():
            wait_in(rows.at[0, other_blocks(c)], sem)

        @pl.when((c < far) & (lax.rem(c, per_plane) != 0))
        def _():
            wait_in(rows.at[0, chunk_rows(c)], sem)

        @pl.when((c >= far) & first)
        def _():
            wait_in(rows.at[:, other_blocks(c)], sem)

        @pl.when((c >= far) & (lax.rem(c, per_plane) != 0))
        def _():
            wait_in(rows.at[:, chunk_rows(c)], sem)

    def own_block(c):
        return pl.ds(pl.multiple_of(c * chunk, chunk), SLOTS)

    def other_blocks(c):
        return pl.ds(pl.multiple_of(c * chunk + SLOTS, SLOTS), chunk - SLOTS)

    def per_chunk(c, yes, no):
        pl.when(c == own_chunk)(yes)
        pl.when(c != own_chunk)(no)

    def first_half(c):
        return pl.ds(pl.multiple_of(c * chunk, chunk), half)

    def second_half(c):
        return pl.ds(pl.multiple_of(c * chunk + half, half), half)

    def x_copies(c):
        here = rows.at[0, chunk_rows(c)]
        return (
            remote(here, rows.at[3, chunk_rows(c)], x_send.at[0, c], x_recv.at[0, c], d, right),
            remote(here, rows.at[1, chunk_rows(c)], x_send.at[1, c], x_recv.at[1, c], d, left),
        )

    def x_relays(c):
        from_left, from_right = rows.at[3, first_half(c)], rows.at[1, second_half(c)]
        return (
            remote(
                from_left, rows.at[2, first_half(c)], x_send.at[2, c], x_recv.at[2, c], d, right
            ),
            remote(
                from_right, rows.at[2, second_half(c)], x_send.at[3, c], x_recv.at[3, c], d, left
            ),
        )

    def h_copies(c):
        here = hid.at[chunk_rows(c), unit_cols(x)]
        return (
            remote(here, here, h_send.at[0, c], h_recv.at[0, c], d, right),
            remote(here, here, h_send.at[1, c], h_recv.at[1, c], d, left),
        )

    def h_relays(c):
        from_left = hid.at[first_half(c), unit_cols(left)]
        from_right = hid.at[second_half(c), unit_cols(right)]
        return (
            remote(from_left, from_left, h_send.at[2, c], h_recv.at[2, c], d, right),
            remote(from_right, from_right, h_send.at[3, c], h_recv.at[3, c], d, left),
        )

    def ret_copy(c, i):
        b = c * per + i
        zz = lax.rem(z - offset(lax.div(b, ny)) + nz, nz)
        return remote(
            outb.at[block_rows(b)], ret.at[block_rows(b)], ret_send.at[c], ret_recv.at[c],
            dev(zz, lax.rem(y - lax.rem(b, ny) + ny, ny)), x,
        )

    def stage_arrive(c):
        moved(c, disp_recv.at[c])
        for copy in x_copies(c):
            copy.start()

    def stage_relay(c):
        wait_in(rows.at[3, chunk_rows(c)], x_recv.at[0, c])
        wait_in(rows.at[1, chunk_rows(c)], x_recv.at[1, c])
        for copy in x_relays(c):
            copy.start()

    def stage_up(i):
        c = entry(CHUNKS, i)

        @pl.when(c < far)
        def _():
            wait_in(rows.at[2, first_half(c)], x_recv.at[2, c])
            wait_in(rows.at[2, second_half(c)], x_recv.at[3, c])

        @pl.when(c >= far)
        def _():
            moved(c, disp_recv.at[c])

        total = jnp.zeros((chunk, 2 * units), f32)
        for j in range(NX):
            features = pl.ds(pl.multiple_of(lax.rem(x + j, NX) * width, width), width)
            total = total + jnp.dot(
                rows[j, chunk_rows(c), :], gu[features, :], preferred_element_type=f32
            )
        gate, up = total[:, :units], total[:, units:]
        hid[chunk_rows(c), unit_cols(x)] = (gate / (1.0 + jnp.exp(-gate)) * up).astype(bf16)
        for copy in h_copies(c):
            copy.start()

    def stage_hid(i):
        c = entry(CHUNKS, i)
        wait_in(hid.at[chunk_rows(c), unit_cols(left)], h_recv.at[0, c])
        wait_in(hid.at[chunk_rows(c), unit_cols(right)], h_recv.at[1, c])
        for copy in h_relays(c):
            copy.start()

    def stage_down(i):
        c = entry(CHUNKS, i)
        wait_in(hid.at[first_half(c), unit_cols(opposite)], h_recv.at[2, c])
        wait_in(hid.at[second_half(c), unit_cols(opposite)], h_recv.at[3, c])
        outb[chunk_rows(c), :] = jnp.dot(
            hid[chunk_rows(c), :], dn[...], preferred_element_type=f32
        ).astype(bf16)
        for i in range(1, per):
            ret_copy(c, i).start()

        def keep():
            ret[own_block(c), :] = outb[own_block(c), :]

        per_chunk(c, keep, lambda: ret_copy(c, 0).start())

    def stage_combine(i):
        at = entry(BACK, i)
        for k in range(per_plane):
            c = at * per_plane + k
            per_chunk(
                c,
                lambda c=c: wait_in(ret.at[other_blocks(c)], ret_recv.at[c]),
                lambda c=c: wait_in(ret.at[chunk_rows(c)], ret_recv.at[c]),
            )
        zz = lax.rem(z + offset(at) + nz, nz)
        sel, taken = chosen(zz, 0, plane, place_ref[...], 0)
        back = ret[pl.ds(pl.multiple_of(at * plane, plane), plane), :]
        total = acc[...]
        for part in (ghi_ref, glo_ref):
            scale = jnp.dot(sel, part[...], preferred_element_type=f32)
            scale = jnp.where(taken, scale, 0.0).astype(bf16)
            total = total + lax.dot_general(
                scale, back, (((0,), (0,)), ((), ())), preferred_element_type=f32
            )
        acc[...] = total

    acc[...] = jnp.zeros_like(acc)

    def head(h, carry):
        scores = jnp.dot(keys[...], query[h], preferred_element_type=f32) * score_scale + bias[...]
        lifted = jnp.exp(scores - jnp.max(scores, axis=0, keepdims=True))
        probs = (lifted / jnp.sum(lifted, axis=0, keepdims=True)).astype(bf16)
        value = lax.dot_general(
            probs, keys[:, :LAT], (((0,), (0,)), ((), ())), preferred_element_type=f32
        )
        for k in range(LAT // LANES):
            wide[k, pl.ds(h, tokens, stride=heads), :] = value[:, k * LANES : (k + 1) * LANES]
        return carry

    def some_heads(first, count):
        lax.fori_loop(first, first + count, head, 0)

    pl.semaphore_wait(barrier, experts - 1 + 4)

    for copy in [t_copy(0, 1), t_copy(1, 1)] + f_own + [lat_copy] + to_side[:2] + to_mate:
        copy.start()
    local_query.wait()
    wait_in(keys.at[pl.ds(0, tokens)], lat_recv.at[0])
    some_heads(0, 4)
    hand_on(1)
    wait_in(wide_tok.at[0, NX - 2], f_recv.at[0])
    wait_in(wide_tok.at[0, 0], f_recv.at[1])
    for copy in f_relays + to_side[2:]:
        copy.start()
    some_heads(4, 4)
    hand_on(2)
    ahead = 4
    for c in range(ahead):
        dispatch(jnp.int32(c))

    attn_copy = pltpu.make_async_copy(attn, attn_ref, q_sem.at[1])

    def step(t, carry):
        def at(delay, stage, count):
            @pl.when((t >= delay) & (t < delay + count))
            def _():
                stage(t - delay)

        at(0, stage_arrive, far)

        @pl.when(t == 0)
        def _():
            hand_on(3)

        @pl.when(t == 1)
        def _():
            wait_in(wide_tok.at[0, 1, upper], f_recv.at[2])
            wait_in(wide_tok.at[0, 1, lower], f_recv.at[3])
            for copy in f_planes:
                copy.start()

        @pl.when(t == 2)
        def _():
            hand_on(middle)

        @pl.when(t == far - ahead)
        def _():
            wait_in(wide_tok.at[1], f_recv.at[4])
            wait_in(wide_tok.at[2], f_recv.at[5])

        @pl.when(t + ahead < chunks)
        def _():
            dispatch(t + ahead)

        at(1, stage_relay, far)

        @pl.when(t == 1)
        def _():
            wait_in(relay_dn.at[0], w_recv.at[4])
            wait_in(relay_dn.at[1], w_recv.at[5])
            for copy in relays:
                copy.start()

        @pl.when(t < 4)
        def _():
            some_heads(8 + 2 * t, 2)

        @pl.when(t == 4)
        def _():
            def narrow(i, carry):
                some = pl.ds(pl.multiple_of(i * tokens, tokens), tokens)
                for k in range(LAT // LANES):
                    attn[some, k * LANES : (k + 1) * LANES] = wide[k, some, :].astype(bf16)
                return carry

            lax.fori_loop(0, heads, narrow, 0)
            attn_copy.start()

        @pl.when(t == 2)
        def _():
            local_gate.wait()
            local_up.wait()
            wait_in(gu.at[mate_in, gate_cols], w_recv.at[0])
            wait_in(gu.at[mate_in, up_cols], w_recv.at[1])

        at(2, stage_up, chunks)
        at(3, stage_hid, chunks)

        @pl.when(t == 3)
        def _():
            local_down.wait()
            wait_in(dn.at[unit_rows(left, 0, units), own_out], w_recv.at[2])
            wait_in(dn.at[unit_rows(right, 0, units), own_out], w_recv.at[3])
            wait_in(dn.at[unit_rows(opposite, 0, halfu), own_out], w_recv.at[6])
            wait_in(dn.at[unit_rows(opposite, halfu, halfu), own_out], w_recv.at[7])
            down_to_mate.start()

        @pl.when(t == 4)
        def _():
            wait_in(dn.at[:, mate_out], w_recv.at[8])

        at(4, stage_down, chunks)

        @pl.when((lax.rem(t, 2) == 0) & (t >= 12) & (t < 12 + 2 * early))
        def _():
            stage_combine(lax.div(t - 12, 2))

        return carry

    early = 3
    lax.fori_loop(0, chunks + 4, step, 0)

    def finish(i, carry):
        stage_combine(i)
        return carry

    lax.fori_loop(early, nz, finish, 0)
    out_ref[...] = acc[...].astype(out_ref.dtype)

    attn_copy.wait()
    lat_copy.wait_send()
    for copy in to_side + to_mate + relays + [down_to_mate] + f_own + f_relays + f_planes:
        copy.wait_send()
    for hop in range(1, middle + 1):
        for way in range(2):
            t_copy(way, hop).wait_send()

    def drain_far(c, carry):
        for copy in x_copies(c) + x_relays(c):
            copy.wait_send()
        return carry

    lax.fori_loop(0, far, drain_far, 0)

    def drain(c, carry):
        for copy in h_copies(c) + h_relays(c):
            copy.wait_send()
        moved(c, disp_send.at[c])
        per_chunk(
            c,
            lambda: wait_in(outb.at[other_blocks(c)], ret_send.at[c]),
            lambda: wait_in(outb.at[chunk_rows(c)], ret_send.at[c]),
        )
        return carry

    lax.fori_loop(0, chunks, drain, 0)


def layer(nz, ny, ids, scores, tok, gate, up, down, query, latent, docs):
    tokens, width = tok.shape
    units = gate.shape[1]
    piece = down.shape[1] // NX
    experts = nz * ny
    count = experts * SLOTS
    chunks = count // CHUNK
    far = chunks * FAR // nz
    heads, feats, _ = query.shape
    vmem = pl.BlockSpec(memory_space=pltpu.VMEM)
    away = pl.BlockSpec(memory_space=pl.ANY)
    bf16 = jnp.bfloat16
    dma = pltpu.SemaphoreType.DMA
    return pl.pallas_call(
        functools.partial(layer_kernel, nz, ny),
        out_shape=(
            jax.ShapeDtypeStruct((tokens, width), bf16),
            jax.ShapeDtypeStruct((tokens * heads, LAT), bf16),
        ),
        in_specs=[vmem, vmem, vmem, away, away, away, away, vmem, vmem],
        out_specs=(vmem, away),
        scratch_shapes=[
            pltpu.VMEM((count, width), bf16),
            pltpu.VMEM((NX - 1, (chunks - far) * CHUNK, width), bf16),
            pltpu.VMEM((nz, tokens, width + LANES), bf16),
            pltpu.VMEM((nz - FAR, NX - 1, tokens, width), bf16),
            pltpu.VMEM((NX, count, width), bf16),
            pltpu.VMEM((NX * width, 2 * units), bf16),
            pltpu.VMEM((NX * units, width), bf16),
            pltpu.VMEM((2, units // 2, piece), bf16),
            pltpu.VMEM((count, NX * units), bf16),
            pltpu.VMEM((count, width), bf16),
            pltpu.VMEM((count, width), bf16),
            pltpu.VMEM((tokens, width), jnp.float32),
            pltpu.VMEM((LANES, tokens), bf16),
            pltpu.VMEM((LANES, tokens), bf16),
            pltpu.VMEM((LANES, tokens), bf16),
            pltpu.VMEM((heads, feats, tokens), bf16),
            pltpu.VMEM((LAT // LANES, tokens * heads, LANES), jnp.float32),
            pltpu.VMEM((tokens * heads, LAT), bf16),
            pltpu.VMEM((2 * tokens, feats), bf16),
            pltpu.VMEM((2 * tokens, tokens), jnp.float32),
            dma((3,)),
            dma((2,)),
            dma((1,)),
            dma((1,)),
            dma((9,)),
            dma((9,)),
            dma((2, nz // 2)),
            dma((2, nz // 2)),
            dma((6,)),
            dma((6,)),
            dma((chunks,)),
            dma((chunks,)),
            dma((4, far)),
            dma((4, far)),
            dma((4, chunks)),
            dma((4, chunks)),
            dma((chunks,)),
            dma((chunks,)),
        ],
        compiler_params=pltpu.CompilerParams(
            collective_id=0, has_side_effects=True, vmem_limit_bytes=58 * 1024 * 1024
        ),
        name="layer",
    )(ids, scores, tok, gate, up, down, query, latent, docs)


def shards(
    queries,
    latents,
    doc_ids,
    hidden_rows,
    expert_ids,
    gate_scores,
    gate_weight,
    up_weight,
    down_weight,
):
    length = lax.axis_size("dp")
    moe_out, attn_out = layer(
        length // (2 * NY),
        NY,
        expert_ids.T,
        gate_scores.T,
        hidden_rows,
        gate_weight[0],
        up_weight[0],
        down_weight[0],
        queries.transpose(1, 2, 0),
        latents.T,
        doc_ids.reshape(length, -1),
    )
    return (attn_out.reshape(queries.shape[:2] + (LAT,)), moe_out)


def solution(mesh):
    placed = (
        P("dp", "mp", None),
        P("dp", None),
        P(),
        P("dp", "mp"),
        P("dp", None),
        P("dp", None),
        P("dp", None, "mp"),
        P("dp", None, "mp"),
        P("dp", "mp", None),
    )
    return jax.shard_map(
        shards,
        mesh=mesh,
        in_specs=placed,
        out_specs=(P("dp", "mp", None), P("dp", "mp")),
        check_vma=False,
    )
```

time: 161 us -> 176 us (1.093); the launches traced: 161 us -> 173 us
  Pallas kernels: 156 us -> 169 us
    pallas_call x1, Pallas kernels: 156 us -> 169 us  [layer(): pl.pallas_call(functools.partial(layer_kernel, nz, ny), out_shape=(jax.Sh...]
where the time goes in v4:
time: 176 us; the launch traced here: 173 us
  Pallas kernels  169 us (96%)
  local copies, waits for them, and re-layouts  3.85 us (2%)
    pallas_call x1, Pallas kernels, layer(): pl.pallas_call(functools.partial(layer_kernel, nz, ny), out_shape=(jax.Sh...  169 us
    unnamed x4, local copies, waits for them, and re-layouts  3.85 us

profile of v4, /device:TPU:16, one launch (start us, length us, event | category | flops | bytes accessed | tf_op | source)
XLA Modules:
  0.0 173.0 jit_solution(1964629447807292406)
XLA Ops:
  0.6 168.5 %layer.1 = (bf16[128,1280]{1,0:T(8,128)(2,1)}, bf16[2048,512]{1,0:T(8,128)(2,1)}) custom-call(s32[6,128]{1,0:T(8,128)} %bitcast.16, f32[6,128]{1,0:T(8,128)} %bitcast.17, bf16[128,1280]{1,0:T(8,128)(2,1)} %tok_ref.1, bf16[2560,384]{1,0:T(8,128)(2,1)} %bitcast.11, bf16[2560,384]{1,0:T(8,128)(2,1)} %bitcast.12, bf16[384,2560]{1,0:T(8,128)(2,1)} %bitcast.13, ...), custom_call_target="tpu_custom_call" | custom-call | tf_op jit(solution)/shard_map/layer/pallas_call | solution.py:697
  169.2 0.0 copy-start
  169.2 3.1 %copy.13 = bf16[128,16,512]{2,1,0:T(8,128)(2,1)} copy(bf16[128,16,512]{2,1,0:T(8,128)(2,1)} %bitcast.10) | data formatting | bytes 4194304
  172.3 0.0 copy-done
  172.3 0.7 copy.14
Async XLA Ops:
  169.2 3.1 %copy-start = (bf16[128,1280]{1,0:T(8,128)(2,1)S(1)}, bf16[128,1280]{1,0:T(8,128)(2,1)}, u32[]{:S(2)}) copy-start(bf16[128,1280]{1,0:T(8,128)(2,1)} %get-tuple-element.9) | copy-start | bytes 983044

commit v5 on v3

--- a/solution.py
+++ b/solution.py
@@ -10,12 +10,13 @@
 
 LAT = 512
 LANES = 128
+PIECES = 8
 SLOTS = 32
 CAP = 30
 CHUNK = 64
 NX = 4
 NY = 4
-Z_ORDER = {8: (0, -2, 4, 3, -3, 2, 1, -1), 4: (0, 2, 1, -1), 2: (0, 1)}
+Z_ORDER = {8: (1, -2, 4, 3, -3, 2, -1, 0), 4: (0, 2, 1, -1), 2: (0, 1)}
 
 score_scale = 1.0 / math.sqrt(192.0)
 neg_large = -1e30
@@ -25,15 +26,15 @@
 def layer_kernel(
     nz,
     ny,
-    ids_ref,
-    score_ref,
-    tok_ref,
+    ids_in,
+    score_in,
+    tok_in,
     gate_ref,
     up_ref,
     down_ref,
     query_ref,
-    latent_ref,
-    doc_ref,
+    latent_in,
+    doc_in,
     out_ref,
     attn_ref,
     disp,
@@ -54,6 +55,12 @@
     attn,
     keys,
     bias,
+    ids_ref,
+    score_ref,
+    tok_ref,
+    latent_ref,
+    doc_ref,
+    in_sem,
     local_sem,
     q_sem,
     lat_send,
@@ -69,9 +76,9 @@
     ret_send,
     ret_recv,
 ):
-    top, tokens = ids_ref.shape
+    top, tokens = ids_in.shape
     heads = query_ref.shape[0]
-    width = tok_ref.shape[1]
+    width = tok_in.shape[1]
     half_in, units = gate_ref.shape
     piece = down_ref.shape[1] // NX
     experts = nz * ny
@@ -131,11 +138,21 @@
     local_down = pltpu.make_async_copy(
         down_ref.at[:, down_cols(x)], dn.at[unit_rows(x, 0, units), own_out], local_sem.at[2]
     )
-    local_gate.start()
-    local_up.start()
-    local_down.start()
     local_query = pltpu.make_async_copy(query_ref, query, q_sem.at[0])
-    local_query.start()
+    inputs = [
+        pltpu.make_async_copy(source, held, in_sem.at[k])
+        for k, (source, held) in enumerate(
+            (
+                (ids_in, ids_ref),
+                (score_in, score_ref),
+                (tok_in, tok_ref),
+                (latent_in, latent_ref),
+                (doc_in, doc_ref),
+            )
+        )
+    ]
+    for copy in inputs:
+        copy.start()
 
     barrier = pltpu.get_barrier_semaphore()
 
@@ -155,6 +172,10 @@
         return carry
 
     lax.fori_loop(1, experts, greet_peer, 0)
+    for copy in [local_gate, local_up, local_down, local_query]:
+        copy.start()
+    for copy in inputs:
+        copy.wait()
 
     expert_at = lax.broadcasted_iota(jnp.int32, (experts, tokens), 0)
     named = jnp.zeros((experts, tokens), f32)
@@ -287,7 +308,7 @@
         per_chunk(c, keep, lambda: disp_copy(c, 0).start())
 
     ahead = min(6, sent)
-    for c in range(2):
+    for c in range(4):
         build(jnp.int32(c))
 
     pl.semaphore_wait(barrier, experts - 1 + 4)
@@ -295,7 +316,7 @@
     for copy in to_side[:2]:
         copy.start()
     for c in range(ahead):
-        if c >= 2:
+        if c >= 4:
             build(jnp.int32(c))
         dispatch(jnp.int32(c))
         if c == 1:
@@ -451,9 +472,9 @@
             wide[k, pl.ds(h, tokens, stride=heads), :] = value[:, k * LANES : (k + 1) * LANES]
         return carry
 
-    parts = min(8, sent)
+    parts = min(4, sent)
     attn_copy = pltpu.make_async_copy(attn, attn_ref, q_sem.at[1])
-    early = min(2, nz)
+    early = min(5, nz)
 
     def step(t, carry):
         def at(delay, stage, count):
@@ -524,9 +545,9 @@
 
         @pl.when(lax.rem(t, 2) == 0)
         def _():
-            @pl.when((t >= 14) & (t < 14 + 2 * early))
+            @pl.when((t >= 10) & (t < 10 + 2 * early))
             def _():
-                stage_combine(lax.div(t - 14, 2))
+                stage_combine(lax.div(t - 10, 2))
 
         return carry
 
@@ -584,7 +605,7 @@
             jax.ShapeDtypeStruct((tokens, width), bf16),
             jax.ShapeDtypeStruct((tokens * heads, LAT), bf16),
         ),
-        in_specs=[vmem, vmem, vmem, away, away, away, away, vmem, vmem],
+        in_specs=[away] * 9,
         out_specs=(vmem, away),
         scratch_shapes=[
             pltpu.VMEM((count, width), bf16),
@@ -605,6 +626,12 @@
             pltpu.VMEM((tokens * heads, LAT), bf16),
             pltpu.VMEM((2 * tokens, feats), bf16),
             pltpu.VMEM((2 * tokens, tokens), jnp.float32),
+            pltpu.VMEM(ids.shape, ids.dtype),
+            pltpu.VMEM(scores.shape, scores.dtype),
+            pltpu.VMEM(tok.shape, tok.dtype),
+            pltpu.VMEM(latent.shape, latent.dtype),
+            pltpu.VMEM(docs.shape, docs.dtype),
+            dma((5,)),
             dma((3,)),
             dma((2,)),
             dma((1,)),
@@ -625,6 +652,45 @@
         ),
         name="layer",
     )(ids, scores, tok, gate, up, down, query, latent, docs)
+
+
+def copy_kernel(first_in, second_in, first_out, second_out, first, second, in_sem, out_sem):
+    rows = first_in.shape[0] // PIECES
+    pieces = []
+    for k in range(PIECES):
+        part = pl.ds(k * rows, rows)
+        pieces.append((first_in.at[part], first.at[part], first_out.at[part]))
+    pieces.append((second_in, second, second_out))
+    into, out = [], []
+    for k, (source, held, target) in enumerate(pieces):
+        into.append(pltpu.make_async_copy(source, held, in_sem.at[k]))
+        out.append(pltpu.make_async_copy(held, target, out_sem.at[k]))
+    for copy in into:
+        copy.start()
+    for arrival, departure in zip(into, out):
+        arrival.wait()
+        departure.start()
+    for copy in out:
+        copy.wait()
+
+
+def handed_over(first, second):
+    away = pl.BlockSpec(memory_space=pl.ANY)
+    dma = pltpu.SemaphoreType.DMA
+    return pl.pallas_call(
+        copy_kernel,
+        out_shape=tuple(jax.ShapeDtypeStruct(a.shape, a.dtype) for a in (first, second)),
+        in_specs=[away, away],
+        out_specs=(away, away),
+        scratch_shapes=[
+            pltpu.VMEM(first.shape, first.dtype),
+            pltpu.VMEM(second.shape, second.dtype),
+            dma((PIECES + 1,)),
+            dma((PIECES + 1,)),
+        ],
+        compiler_params=pltpu.CompilerParams(vmem_limit_bytes=58 * 1024 * 1024),
+        name="handed_over",
+    )(first, second)
 
 
 def shards(
@@ -652,6 +718,7 @@
         latents.T,
         doc_ids.reshape(length, -1),
     )
+    attn_out, moe_out = handed_over(attn_out, moe_out)
     return (attn_out.reshape(queries.shape[:2] + (LAT,)), moe_out)
 
 

time: 161 us -> 160 us (level)
  local copies, waits for them, and re-layouts: 3.85 us -> 0 us
  Pallas kernels: 156 us -> 159 us
    unnamed x4 -> x0, local copies, waits for them, and re-layouts: 3.85 us -> none
    pallas_call x0 -> x1, Pallas kernels: none -> 2.52 us  [handed_over(): pl.pallas_call(copy_kernel, out_shape=tuple((jax.ShapeDtypeStruct(a.shape...]
where the time goes in v5:
time: 160 us
  Pallas kernels  159 us (99%)
    pallas_call x1, Pallas kernels, layer(): pl.pallas_call(functools.partial(layer_kernel, nz, ny), out_shape=(jax.Sh...  157 us

profile of v5, /device:TPU:16, one launch (start us, length us, event | category | flops | bytes accessed | tf_op | source)
XLA Modules:
  0.0 159.7 jit_solution(9059043708398670339)
XLA Ops:
  0.6 156.6 %layer.1 = (bf16[128,1280]{1,0:T(8,128)(2,1)}, bf16[2048,512]{1,0:T(8,128)(2,1)}) custom-call(s32[6,128]{1,0:T(8,128)} %bitcast.15, f32[6,128]{1,0:T(8,128)} %bitcast.16, bf16[128,1280]{1,0:T(8,128)(2,1)} %tok_in.1, bf16[2560,384]{1,0:T(8,128)(2,1)} %bitcast.10, bf16[2560,384]{1,0:T(8,128)(2,1)} %bitcast.11, bf16[384,2560]{1,0:T(8,128)(2,1)} %bitcast.12, ...), custom_call_target="tpu_custom_call" | custom-call | tf_op jit(solution)/shard_map/layer/pallas_call | solution.py:602
  157.2 2.5 %handed_over.1 = (bf16[2048,512]{1,0:T(8,128)(2,1)}, bf16[128,1280]{1,0:T(8,128)(2,1)}) custom-call(bf16[2048,512]{1,0:T(8,128)(2,1)} %get-tuple-element.6.first_in, bf16[128,1280]{1,0:T(8,128)(2,1)} %get-tuple-element.7.second_in), custom_call_target="tpu_custom_call" | custom-call | tf_op jit(solution)/shard_map/handed_over/pallas_call | solution.py:680

commit v6 on v5

--- a/solution.py
+++ b/solution.py
@@ -50,6 +50,7 @@
     place_ref,
     ghi_ref,
     glo_ref,
+    scales,
     query,
     wide,
     attn,
@@ -174,45 +175,6 @@
     lax.fori_loop(1, experts, greet_peer, 0)
     for copy in [local_gate, local_up, local_down, local_query]:
         copy.start()
-    for copy in inputs:
-        copy.wait()
-
-    expert_at = lax.broadcasted_iota(jnp.int32, (experts, tokens), 0)
-    named = jnp.zeros((experts, tokens), f32)
-    weight = jnp.zeros((experts, tokens), f32)
-    for k in range(top):
-        hit = ids_ref[k : k + 1, :] == expert_at
-        named = named + jnp.where(hit, 1.0, 0.0)
-        weight = weight + jnp.where(hit, score_ref[k : k + 1, :], 0.0)
-    row_at = lax.broadcasted_iota(jnp.int32, (tokens, tokens), 0)
-    col_at = lax.broadcasted_iota(jnp.int32, (tokens, tokens), 1)
-    before = jnp.dot(
-        named.astype(bf16),
-        jnp.where(row_at < col_at, 1.0, 0.0).astype(bf16),
-        preferred_element_type=f32,
-    )
-    place_ref[...] = jnp.where(named > 0.5, before, -1.0).astype(bf16)
-    whole = weight.astype(bf16)
-    ghi_ref[...] = whole
-    glo_ref[...] = (weight - whole.astype(f32)).astype(bf16)
-
-    same = row_at == col_at
-    keys[tokens:, :] = lax.dot_general(
-        jnp.where(same, 1.0, 0.0).astype(bf16), latent_ref[...], (((1,), (1,)), ((), ())),
-        preferred_element_type=f32,
-    ).astype(bf16)
-    lat_copy = remote(
-        keys.at[pl.ds(tokens, tokens)], keys.at[pl.ds(0, tokens)],
-        lat_send.at[0], lat_recv.at[0], following, x,
-    )
-    own_ids = doc_ref[pl.ds(d, 1), :]
-    old_ids = doc_ref[pl.ds(lax.rem(d + ring - 1, ring), 1), :]
-    own_col = jnp.sum(jnp.where(same, own_ids, 0).astype(f32), axis=1, keepdims=True)
-    old_col = jnp.sum(jnp.where(same, old_ids, 0).astype(f32), axis=1, keepdims=True)
-    old_col = old_col - jnp.where(d == 0, 1000.0, 0.0)
-    ids_row = own_ids.astype(f32)
-    bias[:tokens, :] = jnp.where(old_col == ids_row, 0.0, neg_large)
-    bias[tokens:, :] = jnp.where((own_col == ids_row) & (row_at <= col_at), 0.0, neg_large)
 
     to_mate = [
         remote(gate_ref, gu.at[own_in, gate_cols], w_send.at[0], w_recv.at[0], mate, x),
@@ -251,6 +213,32 @@
         dn.at[:, own_out], dn.at[:, own_out], w_send.at[8], w_recv.at[8], mate, x
     )
 
+    pl.semaphore_wait(barrier, experts - 1 + 4)
+    for copy in to_side[:2] + to_mate + to_side[2:]:
+        copy.start()
+
+    for copy in inputs:
+        copy.wait()
+
+    expert_at = lax.broadcasted_iota(jnp.int32, (experts, tokens), 0)
+    named = jnp.zeros((experts, tokens), f32)
+    weight = jnp.zeros((experts, tokens), f32)
+    for k in range(top):
+        hit = ids_ref[k : k + 1, :] == expert_at
+        named = named + jnp.where(hit, 1.0, 0.0)
+        weight = weight + jnp.where(hit, score_ref[k : k + 1, :], 0.0)
+    row_at = lax.broadcasted_iota(jnp.int32, (tokens, tokens), 0)
+    col_at = lax.broadcasted_iota(jnp.int32, (tokens, tokens), 1)
+    before = jnp.dot(
+        named.astype(bf16),
+        jnp.where(row_at < col_at, 1.0, 0.0).astype(bf16),
+        preferred_element_type=f32,
+    )
+    place_ref[...] = jnp.where(named > 0.5, before, -1.0).astype(bf16)
+    whole = weight.astype(bf16)
+    ghi_ref[...] = whole
+    glo_ref[...] = (weight - whole.astype(f32)).astype(bf16)
+
     def chunk_rows(c):
         return pl.ds(pl.multiple_of(c * chunk, chunk), chunk)
 
@@ -308,20 +296,28 @@
         per_chunk(c, keep, lambda: disp_copy(c, 0).start())
 
     ahead = min(6, sent)
-    for c in range(4):
+    for c in range(ahead):
         build(jnp.int32(c))
-
-    pl.semaphore_wait(barrier, experts - 1 + 4)
-
-    for copy in to_side[:2]:
-        copy.start()
-    for c in range(ahead):
-        if c >= 4:
-            build(jnp.int32(c))
         dispatch(jnp.int32(c))
-        if c == 1:
-            for copy in to_side[2:] + [lat_copy] + to_mate:
-                copy.start()
+
+    same = row_at == col_at
+    keys[tokens:, :] = lax.dot_general(
+        jnp.where(same, 1.0, 0.0).astype(bf16), latent_ref[...], (((1,), (1,)), ((), ())),
+        preferred_element_type=f32,
+    ).astype(bf16)
+    lat_copy = remote(
+        keys.at[pl.ds(tokens, tokens)], keys.at[pl.ds(0, tokens)],
+        lat_send.at[0], lat_recv.at[0], following, x,
+    )
+    own_ids = doc_ref[pl.ds(d, 1), :]
+    old_ids = doc_ref[pl.ds(lax.rem(d + ring - 1, ring), 1), :]
+    own_col = jnp.sum(jnp.where(same, own_ids, 0).astype(f32), axis=1, keepdims=True)
+    old_col = jnp.sum(jnp.where(same, old_ids, 0).astype(f32), axis=1, keepdims=True)
+    old_col = old_col - jnp.where(d == 0, 1000.0, 0.0)
+    ids_row = own_ids.astype(f32)
+    bias[:tokens, :] = jnp.where(old_col == ids_row, 0.0, neg_large)
+    bias[tokens:, :] = jnp.where((own_col == ids_row) & (row_at <= col_at), 0.0, neg_large)
+    lat_copy.start()
 
     def first_half(c):
         return pl.ds(pl.multiple_of(c * chunk, chunk), half)
@@ -445,17 +441,18 @@
                 lambda c=c: wait_in(ret.at[other_blocks(c)], ret_recv.at[c]),
                 lambda c=c: wait_in(ret.at[chunk_rows(c)], ret_recv.at[c]),
             )
+        back = ret[pl.ds(pl.multiple_of(at * plane, plane), plane), :]
+        total = acc[...]
+        for k in range(2):
+            total = total + jnp.dot(scales[at, k], back, preferred_element_type=f32)
+        acc[...] = total
+
+    def stage_scales(at):
         sel = spread(at, 0, plane)
         taken = chosen(sel)
-        back = ret[pl.ds(pl.multiple_of(at * plane, plane), plane), :]
-        total = acc[...]
-        for part in (ghi_ref, glo_ref):
+        for k, part in enumerate((ghi_ref, glo_ref)):
             scale = jnp.dot(sel, part[...], preferred_element_type=f32)
-            scale = jnp.where(taken, scale, 0.0).astype(bf16)
-            total = total + lax.dot_general(
-                scale, back, (((0,), (0,)), ((), ())), preferred_element_type=f32
-            )
-        acc[...] = total
+            scales[at, k] = jnp.where(taken, scale, 0.0).T.astype(bf16)
 
     hid[:chunk, :] = jnp.zeros((chunk, hid.shape[1]), bf16)
     hid[(packed + 1) * chunk :, :] = jnp.zeros((chunk, hid.shape[1]), bf16)
@@ -498,16 +495,18 @@
             for copy in relays:
                 copy.start()
 
-        @pl.when(t == 0)
+        @pl.when(t == 1)
         def _():
             local_query.wait()
             wait_in(keys.at[pl.ds(0, tokens)], lat_recv.at[0])
 
-        @pl.when(t < parts)
-        def _():
-            lax.fori_loop(t * (heads // parts), (t + 1) * (heads // parts), head, 0)
-
-        @pl.when(t == parts)
+        @pl.when((t >= 1) & (t < 1 + parts))
+        def _():
+            lax.fori_loop((t - 1) * (heads // parts), t * (heads // parts), head, 0)
+
+        at(2, stage_scales, nz)
+
+        @pl.when(t == 1 + parts)
         def _():
             def narrow(i, carry):
                 some = pl.ds(pl.multiple_of(i * tokens, tokens), tokens)
@@ -621,6 +620,7 @@
             pltpu.VMEM((experts, tokens), bf16),
             pltpu.VMEM((experts, tokens), bf16),
             pltpu.VMEM((experts, tokens), bf16),
+            pltpu.VMEM((nz, 2, tokens, ny * SLOTS), bf16),
             pltpu.VMEM((heads, feats, tokens), bf16),
             pltpu.VMEM((LAT // LANES, tokens * heads, LANES), jnp.float32),
             pltpu.VMEM((tokens * heads, LAT), bf16),

time: 160 us -> 161 us (level)
  no operation moved by 1% of the time
where the time goes in v6:
time: 161 us; the launch traced here: 160 us
  Pallas kernels  160 us (99%)
    pallas_call x1, Pallas kernels, layer(): pl.pallas_call(functools.partial(layer_kernel, nz, ny), out_shape=(jax.Sh...  157 us

profile of v6, /device:TPU:16, one launch (start us, length us, event | category | flops | bytes accessed | tf_op | source)
XLA Modules:
  0.0 160.2 jit_solution(7154640867615468141)
XLA Ops:
  0.6 157.0 %layer.1 = (bf16[128,1280]{1,0:T(8,128)(2,1)}, bf16[2048,512]{1,0:T(8,128)(2,1)}) custom-call(s32[6,128]{1,0:T(8,128)} %bitcast.15, f32[6,128]{1,0:T(8,128)} %bitcast.16, bf16[128,1280]{1,0:T(8,128)(2,1)} %tok_in.1, bf16[2560,384]{1,0:T(8,128)(2,1)} %bitcast.10, bf16[2560,384]{1,0:T(8,128)(2,1)} %bitcast.11, bf16[384,2560]{1,0:T(8,128)(2,1)} %bitcast.12, ...), custom_call_target="tpu_custom_call" | custom-call | tf_op jit(solution)/shard_map/layer/pallas_call | solution.py:601
  157.7 2.5 %handed_over.1 = (bf16[2048,512]{1,0:T(8,128)(2,1)}, bf16[128,1280]{1,0:T(8,128)(2,1)}) custom-call(bf16[2048,512]{1,0:T(8,128)(2,1)} %get-tuple-element.6.first_in, bf16[128,1280]{1,0:T(8,128)(2,1)} %get-tuple-element.7.second_in), custom_call_target="tpu_custom_call" | custom-call | tf_op jit(solution)/shard_map/handed_over/pallas_call | solution.py:680

commit v7 on v6

--- a/solution.py
+++ b/solution.py
@@ -13,10 +13,15 @@
 PIECES = 8
 SLOTS = 32
 CAP = 30
+SLOT_BITS = 5
+CAP_TIMES, CAP_SHIFT = 34953, 20
+assert all(n * CAP_TIMES >> CAP_SHIFT == n // CAP for n in range(2048))
 CHUNK = 64
 NX = 4
 NY = 4
-Z_ORDER = {8: (1, -2, 4, 3, -3, 2, -1, 0), 4: (0, 2, 1, -1), 2: (0, 1)}
+COMBINE_AT = ((10, 0), (13, 1), (17, 3))
+COMBINE_LAST = (2, 4, 5, 6, 7)
+Z_ORDER = {8: (1, -2, 4, 2, -3, 3, -1, 0), 4: (0, 2, 1, -1), 2: (0, 1)}
 
 score_scale = 1.0 / math.sqrt(192.0)
 neg_large = -1e30
@@ -104,11 +109,14 @@
     def dev(zz, yy):
         return (zz * ny + yy) * 2 + s
 
-    def offset(c):
+    def entry(table, i):
         total = 0
-        for at, by in enumerate(Z_ORDER[nz]):
-            total = total + jnp.where(c == at, by, 0)
+        for at, value in enumerate(table):
+            total = total + jnp.where(i == at, value, 0)
         return total
+
+    def offset(at):
+        return entry(Z_ORDER[nz], at)
 
     def remote(src, dst, send, recv, dd, xx):
         return pltpu.make_async_remote_copy(
@@ -252,14 +260,14 @@
     def spread(at, first, count):
         zz = lax.rem(z + offset(at) + nz, nz)
         row = lax.broadcasted_iota(jnp.int32, (count, experts), 0)
-        dest = zz * ny + ((y + first + (row // SLOTS)) % ny)
+        dest = zz * ny + ((y + first + (row >> SLOT_BITS)) & (ny - 1))
         return jnp.where(
             lax.broadcasted_iota(jnp.int32, (count, experts), 1) == dest, 1.0, 0.0
         ).astype(bf16)
 
     def chosen(sel):
         count = sel.shape[0]
-        slot = (lax.broadcasted_iota(jnp.int32, (count, tokens), 0) % SLOTS).astype(f32)
+        slot = (lax.broadcasted_iota(jnp.int32, (count, tokens), 0) & (SLOTS - 1)).astype(f32)
         return jnp.dot(sel, place_ref[...], preferred_element_type=f32) == slot
 
     def build(c):
@@ -376,7 +384,8 @@
         arrived(c + 1)
         row = lax.broadcasted_iota(jnp.int32, (chunk, 2 * chunk), 0)
         col = lax.broadcasted_iota(jnp.int32, (chunk, 2 * chunk), 1)
-        take = col == row + (SLOTS - CAP) * ((row + c * chunk) // CAP)
+        block = ((row + c * chunk) * CAP_TIMES) >> CAP_SHIFT
+        take = col == row + (SLOTS - CAP) * block
         window = land[pl.ds(pl.multiple_of(c * chunk, chunk), 2 * chunk), :]
         rows[x, chunk_rows(c), :] = jnp.dot(
             jnp.where(take, 1.0, 0.0).astype(bf16), window, preferred_element_type=f32
@@ -419,7 +428,8 @@
         row = lax.broadcasted_iota(jnp.int32, (chunk, 2 * chunk), 0)
         col = lax.broadcasted_iota(jnp.int32, (chunk, 2 * chunk), 1)
         place = c * chunk + row
-        take = (col + (c - 1) * chunk == place - (SLOTS - CAP) * (place // SLOTS)) & (row % SLOTS < CAP)
+        held = place - (SLOTS - CAP) * (place >> SLOT_BITS)
+        take = (col + (c - 1) * chunk == held) & ((row & (SLOTS - 1)) < CAP)
         window = hid[pl.ds(pl.multiple_of(c * chunk, chunk), 2 * chunk), :]
         value = jnp.dot(
             jnp.where(take, 1.0, 0.0).astype(bf16), window, preferred_element_type=f32
@@ -471,7 +481,6 @@
 
     parts = min(4, sent)
     attn_copy = pltpu.make_async_copy(attn, attn_ref, q_sem.at[1])
-    early = min(5, nz)
 
     def step(t, carry):
         def at(delay, stage, count):
@@ -542,21 +551,21 @@
 
         at(4, stage_down, sent)
 
-        @pl.when(lax.rem(t, 2) == 0)
-        def _():
-            @pl.when((t >= 10) & (t < 10 + 2 * early))
-            def _():
-                stage_combine(lax.div(t - 10, 2))
+        for moment, k in COMBINE_AT:
+
+            @pl.when(t == moment)
+            def _(k=k):
+                stage_combine(jnp.int32(k))
 
         return carry
 
     lax.fori_loop(0, sent + 4, step, 0)
 
-    def finish(at, carry):
-        stage_combine(at)
+    def finish(i, carry):
+        stage_combine(entry(COMBINE_LAST, i))
         return carry
 
-    lax.fori_loop(early, nz, finish, 0)
+    lax.fori_loop(0, len(COMBINE_LAST), finish, 0)
     out_ref[...] = acc[...].astype(out_ref.dtype)
 
     attn_copy.wait()

time: 161 us -> 160 us (level)
  no operation moved by 1% of the time
where the time goes in v7:
time: 160 us; the launch traced here: 159 us
  Pallas kernels  159 us (99%)
    pallas_call x1, Pallas kernels, layer(): pl.pallas_call(functools.partial(layer_kernel, nz, ny), out_shape=(jax.Sh...  156 us

profile of v7, /device:TPU:16, one launch (start us, length us, event | category | flops | bytes accessed | tf_op | source)
XLA Modules:
  0.0 159.3 jit_solution(13934341350581523993)
XLA Ops:
  0.6 156.1 %layer.1 = (bf16[128,1280]{1,0:T(8,128)(2,1)}, bf16[2048,512]{1,0:T(8,128)(2,1)}) custom-call(s32[6,128]{1,0:T(8,128)} %bitcast.15, f32[6,128]{1,0:T(8,128)} %bitcast.16, bf16[128,1280]{1,0:T(8,128)(2,1)} %tok_in.1, bf16[2560,384]{1,0:T(8,128)(2,1)} %bitcast.10, bf16[2560,384]{1,0:T(8,128)(2,1)} %bitcast.11, bf16[384,2560]{1,0:T(8,128)(2,1)} %bitcast.12, ...), custom_call_target="tpu_custom_call" | custom-call | tf_op jit(solution)/shard_map/layer/pallas_call | solution.py:610
  156.8 2.5 %handed_over.1 = (bf16[2048,512]{1,0:T(8,128)(2,1)}, bf16[128,1280]{1,0:T(8,128)(2,1)}) custom-call(bf16[2048,512]{1,0:T(8,128)(2,1)} %get-tuple-element.6.first_in, bf16[128,1280]{1,0:T(8,128)(2,1)} %get-tuple-element.7.second_in), custom_call_target="tpu_custom_call" | custom-call | tf_op jit(solution)/shard_map/handed_over/pallas_call | solution.py:689

commit v8 on v7

--- a/solution.py
+++ b/solution.py
@@ -19,9 +19,9 @@
 CHUNK = 64
 NX = 4
 NY = 4
-COMBINE_AT = ((10, 0), (13, 1), (17, 3))
-COMBINE_LAST = (2, 4, 5, 6, 7)
-Z_ORDER = {8: (1, -2, 4, 2, -3, 3, -1, 0), 4: (0, 2, 1, -1), 2: (0, 1)}
+COMBINE_AT = ((10, 0), (12, 1), (14, 2), (16, 3), (18, 4))
+COMBINE_LAST = (5, 6, 7)
+Z_ORDER = {8: (1, -2, 4, 3, -3, 2, -1, 0), 4: (0, 2, 1, -1), 2: (0, 1)}
 
 score_scale = 1.0 / math.sqrt(192.0)
 neg_large = -1e30
@@ -482,6 +482,29 @@
     parts = min(4, sent)
     attn_copy = pltpu.make_async_copy(attn, attn_ref, q_sem.at[1])
 
+    def drain_x(c):
+        for copy in x_copies(c) + x_relays(c):
+            copy.wait_send()
+
+    def drain_h(c):
+        for copy in h_copies(c) + h_relays(c):
+            copy.wait_send()
+
+    def drain_disp(c):
+        per_chunk(
+            c,
+            lambda: wait_in(disp.at[other_blocks(c)], disp_send.at[c]),
+            lambda: wait_in(disp.at[chunk_rows(c)], disp_send.at[c]),
+        )
+
+    def drain_ret(c, carry=0):
+        per_chunk(
+            c,
+            lambda: wait_in(outb.at[other_blocks(c)], ret_send.at[c]),
+            lambda: wait_in(outb.at[chunk_rows(c)], ret_send.at[c]),
+        )
+        return carry
+
     def step(t, carry):
         def at(delay, stage, count):
             @pl.when((t >= delay) & (t < delay + count))
@@ -551,6 +574,18 @@
 
         at(4, stage_down, sent)
 
+        at(6, drain_x, packed)
+        at(7, drain_h, packed)
+        at(4, drain_disp, sent)
+        at(10, drain_ret, sent)
+
+        @pl.when(t == 12)
+        def _():
+            attn_copy.wait()
+            lat_copy.wait_send()
+            for copy in to_side + to_mate + relays + [down_to_mate]:
+                copy.wait_send()
+
         for moment, k in COMBINE_AT:
 
             @pl.when(t == moment)
@@ -560,6 +595,10 @@
         return carry
 
     lax.fori_loop(0, sent + 4, step, 0)
+    for c in range(sent + 4 - 6, packed):
+        drain_x(c)
+    for c in range(sent + 4 - 7, packed):
+        drain_h(c)
 
     def finish(i, carry):
         stage_combine(entry(COMBINE_LAST, i))
@@ -567,32 +606,7 @@
 
     lax.fori_loop(0, len(COMBINE_LAST), finish, 0)
     out_ref[...] = acc[...].astype(out_ref.dtype)
-
-    attn_copy.wait()
-    lat_copy.wait_send()
-    for copy in to_side + to_mate + relays + [down_to_mate]:
-        copy.wait_send()
-
-    def drain(c, carry):
-        for copy in x_copies(c) + x_relays(c) + h_copies(c) + h_relays(c):
-            copy.wait_send()
-        return carry
-
-    lax.fori_loop(0, packed, drain, 0)
-
-    def drain_sent(c, carry):
-        def some():
-            wait_in(disp.at[other_blocks(c)], disp_send.at[c])
-            wait_in(outb.at[other_blocks(c)], ret_send.at[c])
-
-        def whole():
-            wait_in(disp.at[chunk_rows(c)], disp_send.at[c])
-            wait_in(outb.at[chunk_rows(c)], ret_send.at[c])
-
-        per_chunk(c, some, whole)
-        return carry
-
-    lax.fori_loop(0, sent, drain_sent, 0)
+    lax.fori_loop(sent + 4 - 10, sent, drain_ret, 0)
 
 
 def layer(nz, ny, ids, scores, tok, gate, up, down, query, latent, docs):

time: 160 us -> 160 us (level)
  no operation moved by 1% of the time
where the time goes in v8:
time: 160 us
  Pallas kernels  159 us (99%)
    pallas_call x1, Pallas kernels, layer(): pl.pallas_call(functools.partial(layer_kernel, nz, ny), out_shape=(jax.Sh...  157 us

profile of v8, /device:TPU:16, one launch (start us, length us, event | category | flops | bytes accessed | tf_op | source)
XLA Modules:
  0.0 160.0 jit_solution(18389740914529353515)
XLA Ops:
  0.6 156.8 %layer.1 = (bf16[128,1280]{1,0:T(8,128)(2,1)}, bf16[2048,512]{1,0:T(8,128)(2,1)}) custom-call(s32[6,128]{1,0:T(8,128)} %bitcast.15, f32[6,128]{1,0:T(8,128)} %bitcast.16, bf16[128,1280]{1,0:T(8,128)(2,1)} %tok_in.1, bf16[2560,384]{1,0:T(8,128)(2,1)} %bitcast.10, bf16[2560,384]{1,0:T(8,128)(2,1)} %bitcast.11, bf16[384,2560]{1,0:T(8,128)(2,1)} %bitcast.12, ...), custom_call_target="tpu_custom_call" | custom-call | tf_op jit(solution)/shard_map/layer/pallas_call | solution.py:624
  157.4 2.5 %handed_over.1 = (bf16[2048,512]{1,0:T(8,128)(2,1)}, bf16[128,1280]{1,0:T(8,128)(2,1)}) custom-call(bf16[2048,512]{1,0:T(8,128)(2,1)} %get-tuple-element.6.first_in, bf16[128,1280]{1,0:T(8,128)(2,1)} %get-tuple-element.7.second_in), custom_call_target="tpu_custom_call" | custom-call | tf_op jit(solution)/shard_map/handed_over/pallas_call | solution.py:703

commit v9 on v5

--- a/solution.py
+++ b/solution.py
@@ -622,7 +622,7 @@
             pltpu.VMEM((experts, tokens), bf16),
             pltpu.VMEM((experts, tokens), bf16),
             pltpu.VMEM((heads, feats, tokens), bf16),
-            pltpu.VMEM((LAT // LANES, tokens * heads, LANES), jnp.float32),
+            pltpu.VMEM((LAT // LANES, (tokens + 1) * heads, LANES), jnp.float32),
             pltpu.VMEM((tokens * heads, LAT), bf16),
             pltpu.VMEM((2 * tokens, feats), bf16),
             pltpu.VMEM((2 * tokens, tokens), jnp.float32),

time: 160 us -> 160 us (level)
  no operation moved by 1% of the time
where the time goes in v9:
time: 160 us
  Pallas kernels  159 us (99%)
    pallas_call x1, Pallas kernels, layer(): pl.pallas_call(functools.partial(layer_kernel, nz, ny), out_shape=(jax.Sh...  157 us

profile of v9, /device:TPU:16, one launch (start us, length us, event | category | flops | bytes accessed | tf_op | source)
XLA Modules:
  0.0 159.7 jit_solution(16058953112913196834)
XLA Ops:
  0.6 156.6 %layer.1 = (bf16[128,1280]{1,0:T(8,128)(2,1)}, bf16[2048,512]{1,0:T(8,128)(2,1)}) custom-call(s32[6,128]{1,0:T(8,128)} %bitcast.15, f32[6,128]{1,0:T(8,128)} %bitcast.16, bf16[128,1280]{1,0:T(8,128)(2,1)} %tok_in.1, bf16[2560,384]{1,0:T(8,128)(2,1)} %bitcast.10, bf16[2560,384]{1,0:T(8,128)(2,1)} %bitcast.11, bf16[384,2560]{1,0:T(8,128)(2,1)} %bitcast.12, ...), custom_call_target="tpu_custom_call" | custom-call | tf_op jit(solution)/shard_map/layer/pallas_call | solution.py:602
  157.2 2.5 %handed_over.1 = (bf16[2048,512]{1,0:T(8,128)(2,1)}, bf16[128,1280]{1,0:T(8,128)(2,1)}) custom-call(bf16[2048,512]{1,0:T(8,128)(2,1)} %get-tuple-element.6.first_in, bf16[128,1280]{1,0:T(8,128)(2,1)} %get-tuple-element.7.second_in), custom_call_target="tpu_custom_call" | custom-call | tf_op jit(solution)/shard_map/handed_over/pallas_call | solution.py:680
